TPU v7x, 256 devices: a whole 4x4x8 slice. The times are simulated.
256 devices in a mesh: depth: 2 (over y_hi), row: 16 (over x, y_lo, core), col: 8 (over z).
Axes of the slice: x: 4, y: 4 (y_hi: 2, y_lo: 2; y = y_hi * 2 + y_lo), z: 8, core: 2. Of those that a mesh axis runs over, the one named last changes fastest.
Arguments:
- volume: bfloat16 [64, 256, 8192], P('depth', 'row', 'col'), may hold values from -6 to 6
- first_weight: bfloat16 [64, 864], replicated, may hold values from -0.21875 to 0.21875
- second_weight: bfloat16 [128, 1728], replicated, may hold values from -0.15625 to 0.15625
- cotangent: bfloat16 [16, 64, 8192], P('depth', 'row', 'col'), may hold values from -0.011962891 to 0.011962891
Outputs:
- first_grad: float32 [64, 864], replicated
- second_grad: float32 [128, 1728], replicated
All inputs are finite; a program needn't handle non-finite values.
Results may differ from a plain program's by a relative error of at most 0.0047.
Values may be sent and summed in bfloat16 or wider, within the bound.
A program may use at most 128 MiB of HBM per device.

v0:
```python
import jax
import jax.numpy as jnp
from jax import lax
from jax.experimental import pallas as pl
from jax.experimental.pallas import tpu as pltpu
from jax.sharding import PartitionSpec as P

MESH = pl.DeviceIdType.MESH
F32 = jnp.float32
BF16 = jnp.bfloat16

ROWS = 2304
LINK = BF16


def leaky(values):
    root = lax.rsqrt(values * values + 1.0)
    return 0.6 * values + 0.4 * ((values * values + 1.0) * root - 1.0)


def leaky_slope(values):
    return 0.6 + 0.4 * values * lax.rsqrt(values * values + 1.0)


def dot_nt(lhs, rhs):
    return lax.dot_general(lhs, rhs, (((1,), (1,)), ((), ())), preferred_element_type=F32)


def dot_nn(lhs, rhs):
    return lax.dot_general(lhs, rhs, (((1,), (0,)), ((), ())), preferred_element_type=F32)


def window(ref, *lead):
    low = ref[lead + (pl.ds(0, 8),)].reshape(256, 128)
    high = ref[lead + (pl.ds(1, 8),)].reshape(256, 128)
    return jnp.concatenate([low, high], axis=1)


def make_kernel(n_dep, n_row, n_col):
    n_half = n_row // 2
    n_plane = n_dep * n_half
    chunk = ROWS // (2 * n_plane)
    piece = chunk // n_col

    def kernel(
        vol, w1, w2, cot, g1_out, g2_out,
        s_ref, f_ref, w1f, w2f, w1b, w2b, up,
        sr, f_c, f_r, f_d, f_dc, f_dr, f_drc,
        hs, hx, slope1, h_sc, h_sr, h_sd, h_c, h_r, h_d, h_dr,
        q_ref, dx, d2t, d1t, q_sc, q_sr, q_sd, q_c, q_r, q_d, q_dr,
        acc, half, send1, recv1, send2, recv2, part, send3, recv3, tot, recv4, gath, full,
        halo_send, halo_recv, sum_send, sum_recv,
    ):
        dep, row, col = lax.axis_index("depth"), lax.axis_index("row"), lax.axis_index("col")
        core, line = lax.rem(row, 2), lax.div(row, 2)
        plane = dep * n_half + line

        def plane_dev(index):
            return (lax.div(index, n_half), 2 * lax.rem(index, n_half) + core, col)

        def shifted(step, d, r, c):
            return (
                lax.rem(dep + d * step + n_dep, n_dep),
                lax.rem(row + r * step + n_row, n_row),
                lax.rem(col + c * step + n_col, n_col),
            )

        mate = (dep, row + 1 - 2 * core, col)
        corners = [(d, r, c) for d in (0, 1) for r in (0, 1) for c in (0, 1)][1:]

        barrier = pltpu.get_barrier_semaphore()
        peers = [shifted(s, *e) for e in corners for s in (1, -1)]
        peers.append(mate)
        peers += [plane_dev(lax.rem(plane + s, n_plane)) for s in range(1, n_plane)]
        peers += [(dep, row, lax.rem(col + s, n_col)) for s in range(1, n_col)]
        for peer in peers:
            pl.semaphore_signal(barrier, inc=1, device_id=peer, device_id_type=MESH)

        for rd in range(4):
            for t in range(8):
                s_ref[rd, 1 + t, pl.ds(24, 128), :] = (
                    vol[:, rd, :, pl.ds(128 * t, 128)].astype(F32).reshape(128, 128)
                )
        for t in range(8):
            rows = [s_ref[rd, 1 + t, pl.ds(24 + 15, 8, stride=16), :] for rd in range(4)]
            sr[t] = jnp.concatenate(rows, axis=0).astype(BF16)

        pl.semaphore_wait(barrier, len(peers))

        def halo(phase, kind, src, dst, step):
            index = phase * 7 + kind
            return pltpu.make_async_remote_copy(
                src_ref=src, dst_ref=dst, send_sem=halo_send.at[index], recv_sem=halo_recv.at[index],
                device_id=shifted(step, *corners[kind]), device_id_type=MESH,
            )

        tail = pl.ds(896, 128)
        field_copies = [
            halo(0, 0, vol.at[:, :, :, tail], f_c, 1),
            halo(0, 1, sr, f_r.at[pl.ds(1, 8)], 1),
            halo(0, 2, sr.at[7], f_r.at[0], 1),
            halo(0, 3, vol.at[7, 3], f_d, 1),
            halo(0, 4, vol.at[7, 3, :, tail], f_dc, 1),
            halo(0, 5, vol.at[7, 3], f_dr, 1),
            halo(0, 6, vol.at[7, 3, :, tail], f_drc, 1),
        ]
        for copy in field_copies:
            copy.start()

        w1f[:, pl.ds(768, 128)] = jnp.zeros((64, 128), F32)
        w1f[:, pl.ds(0, 864)] = w1[...].astype(F32)
        w2f[:, pl.ds(1664, 128)] = jnp.zeros((128, 128), F32)
        w2f[:, pl.ds(0, 1728)] = w2[...].astype(F32)
        lane1 = lax.broadcasted_iota(jnp.int32, (64, 256), 1)
        lane2 = lax.broadcasted_iota(jnp.int32, (128, 256), 1)
        for ab in range(9):
            tile, off = divmod(ab * 96, 128)
            if tile == 6:
                band = jnp.concatenate([w1f[:, pl.ds(768, 128)], jnp.zeros((64, 128), F32)], axis=1)
            else:
                band = w1f[:, pl.ds(128 * tile, 256)]
            for kk, start in ((0, 96), (1, 160)):
                moved = pltpu.roll(band, (start - off) % 256, 1)
                keep = (lane1 >= start) & (lane1 < start + 96)
                w1b[ab, pl.ds(64 * kk, 64), :] = jnp.where(keep, moved, 0.0).astype(BF16)
            tile, off = divmod(ab * 192, 128)
            band = w2f[:, pl.ds(128 * tile, 256)]
            moved = band if off == 64 else pltpu.roll(band, 64, 1)
            w2b[ab] = jnp.where(lane2 >= 64, moved, 0.0).astype(BF16)
        for i in range(8):
            line_up = cot[i].astype(F32)
            for k in range(8):
                up[k, pl.ds(4 * i, 4), :] = line_up[:, 128 * k : 128 * (k + 1)]

        def pick_field(t, rd, rr):
            source, start = (3, 8) if rd < 0 else (rd, 24)
            rows = s_ref[source, t, pl.ds(start + rr, 32, stride=4), :]
            f_ref[rd + 1, rr + 1, t] = rows.astype(BF16)

        def local_tile(t, carry):
            for rd in range(4):
                for rr in range(4):
                    pick_field(t, rd, rr)
            return carry

        lax.fori_loop(1, 9, local_tile, 0)

        for copy in field_copies:
            copy.wait()

        first_dep, first_row, first_col = dep == 0, row == 0, col == 0

        def unless(edge, values):
            return jnp.where(edge, 0.0, values.astype(F32))

        for rd in range(4):
            s_ref[rd, 0, pl.ds(24, 128), :] = unless(first_col, f_c[:, rd]).reshape(128, 128)
        for t in range(8):
            s_ref[3, 1 + t, pl.ds(8, 16), :] = unless(first_dep, f_d[:, pl.ds(128 * t, 128)])
        s_ref[3, 0, pl.ds(8, 16), :] = unless(first_dep | first_col, f_dc[...])
        for rd in range(4):
            for rr in range(4):
                pick_field(0, rd, rr)

        def above_tile(t, carry):
            for rr in range(4):
                pick_field(t, -1, rr)
            return carry

        lax.fori_loop(0, 9, above_tile, 0)

        def row_tile(t, carry):
            block = unless(first_row | (first_col & (t == 0)), f_r[t])
            for rd in range(4):
                s_ref[rd, t, pl.ds(23, 8, stride=16), :] = block[8 * rd : 8 * rd + 8]
            return carry

        lax.fori_loop(0, 9, row_tile, 0)
        for t in range(9):
            block = f_drc[...] if t == 0 else f_dr[:, pl.ds(128 * (t - 1), 128)]
            edge = first_dep | first_row
            edge = edge | first_col if t == 0 else edge
            s_ref[3, t, pl.ds(7, 1), :] = unless(edge, block)[15:16]

        def behind_tile(t, carry):
            for rd in range(-1, 4):
                pick_field(t, rd, -1)
            return carry

        lax.fori_loop(0, 9, behind_tile, 0)

        for pd in range(2):
            for pr in range(2):
                pre = jnp.zeros((256, 128), F32)
                for ab in range(9):
                    a, b = divmod(ab, 3)
                    pre += dot_nt(window(f_ref, 2 * pd + a, 2 * pr + b), w1b[ab])
                slope1[pd, pr] = leaky_slope(pre)
                hid = leaky(pre).reshape(8, 32, 128)
                hs[pd, pr, pl.ds(1, 8), pl.ds(8, 32), :] = hid
                h_sc[2 * pd + pr] = hid[7].astype(BF16)
        for t in range(8):
            rows = [hs[pd, 1, 1 + t, pl.ds(11, 8, stride=4), :] for pd in range(2)]
            h_sr[t] = jnp.concatenate(rows, axis=0).astype(BF16)
            rows = [hs[1, pr, 1 + t, pl.ds(32, 8), :] for pr in range(2)]
            h_sd[t] = jnp.concatenate(rows, axis=0).astype(BF16)
        hidden_copies = [
            halo(1, 0, h_sc, h_c, 1),
            halo(1, 1, h_sr, h_r.at[pl.ds(1, 8)], 1),
            halo(1, 2, h_sr.at[7], h_r.at[0], 1),
            halo(1, 3, h_sd, h_d.at[pl.ds(1, 8)], 1),
            halo(1, 4, h_sd.at[7], h_d.at[0], 1),
            halo(1, 5, h_sd, h_dr.at[pl.ds(1, 8)], 1),
            halo(1, 6, h_sd.at[7], h_dr.at[0], 1),
        ]
        for copy in hidden_copies:
            copy.start()
        for copy in hidden_copies:
            copy.wait()
        for pd in range(2):
            for pr in range(2):
                hs[pd, pr, 0, pl.ds(8, 32), :] = unless(first_col, h_c[2 * pd + pr])
        for t in range(9):
            edge = first_dep | first_col if t == 0 else first_dep
            block = unless(edge, h_d[t])
            for pr in range(2):
                hs[1, pr, t, pl.ds(4, 4), :] = block[8 * pr + 4 : 8 * pr + 8]

        def pick_hidden(a, b, pd, pr, start):
            hx[3 * a + b] = hs[pd, pr, :, pl.ds(start, 32), :].astype(BF16)

        for pr in range(2):
            pick_hidden(0, 1 + pr, 1, pr, 4)
            pick_hidden(1, 1 + pr, 0, pr, 8)
            pick_hidden(2, 1 + pr, 1, pr, 8)
        for t in range(9):
            edge = first_row | first_col if t == 0 else first_row
            block = unless(edge, h_r[t])
            for pd in range(2):
                hs[pd, 1, t, pl.ds(7, 8, stride=4), :] = block[8 * pd : 8 * pd + 8]
            block = unless(edge | first_dep, h_dr[t])
            hs[1, 1, t, pl.ds(3, 1), :] = block[15:16]
        pick_hidden(0, 0, 1, 1, 3)
        pick_hidden(1, 0, 0, 1, 7)
        pick_hidden(2, 0, 1, 1, 7)

        pre = jnp.zeros((256, 128), F32)
        for ab in range(9):
            pre += dot_nt(window(hx, ab), w2b[ab])
        delta2 = up[...].reshape(256, 128) * leaky_slope(pre)
        q_ref[pl.ds(0, 8), pl.ds(0, 32), :] = delta2.reshape(8, 32, 128)
        q_sc[...] = delta2[:32].astype(BF16)
        for t in range(8):
            q_sr[t] = q_ref[t, pl.ds(0, 8, stride=4), :]
            q_sd[t] = q_ref[t, pl.ds(0, 8), :]
        delta_copies = [
            halo(2, 0, q_sc, q_c, -1),
            halo(2, 1, q_sr, q_r.at[pl.ds(0, 8)], -1),
            halo(2, 2, q_sr.at[0], q_r.at[8], -1),
            halo(2, 3, q_sd, q_d.at[pl.ds(0, 8)], -1),
            halo(2, 4, q_sd.at[0], q_d.at[8], -1),
            halo(2, 5, q_sd, q_dr.at[pl.ds(0, 8)], -1),
            halo(2, 6, q_sd.at[0], q_dr.at[8], -1),
        ]
        for copy in delta_copies:
            copy.start()

        d2t[...] = delta2.T.astype(BF16)
        lane = lax.broadcasted_iota(jnp.int32, (128, 128), 1)
        held = None
        for ab in range(9):
            grad = dot_nn(d2t[...], window(hx, ab))
            left, right = grad[:, :128], grad[:, 128:]
            tile = 3 * (ab // 2)
            if ab % 2 == 0:
                acc[pl.ds(128 * tile, 128), :] = pltpu.roll(jnp.where(lane >= 64, left, right), 64, 1)
                held = pltpu.roll(right, 64, 1)
            else:
                acc[pl.ds(128 * tile + 128, 128), :] = jnp.where(lane < 64, held, left)
                acc[pl.ds(128 * tile + 256, 128), :] = right
        acc[pl.ds(128 * 13, 128), :] = held

        for copy in delta_copies:
            copy.wait()
        last_dep, last_row, last_col = dep == n_dep - 1, row == n_row - 1, col == n_col - 1
        q_ref[8, pl.ds(0, 32), :] = unless(last_col, q_c[...])
        for t in range(9):
            edge = last_dep | last_col if t == 8 else last_dep
            q_ref[t, pl.ds(32, 4), :] = unless(edge, q_d[t])[:4]
        dx[0] = q_ref[:, pl.ds(0, 32), :].astype(BF16)
        dx[2] = q_ref[:, pl.ds(4, 32), :].astype(BF16)
        for t in range(9):
            edge = last_row | last_col if t == 8 else last_row
            q_ref[t, pl.ds(4, 8, stride=4), :] = unless(edge, q_r[t])
            q_ref[t, pl.ds(36, 1), :] = unless(edge | last_dep, q_dr[t])[:1]
        dx[1] = q_ref[:, pl.ds(1, 32), :].astype(BF16)
        dx[3] = q_ref[:, pl.ds(5, 32), :].astype(BF16)

        taps = (((1, 0),), ((2, 0), (0, 1)))
        for pd in range(2):
            for pr in range(2):
                back = jnp.zeros((256, 128), F32)
                for a, od in taps[pd]:
                    for b, o_r in taps[pr]:
                        band = w2b[3 * a + b]
                        band = jnp.concatenate([band[:, 128:], band[:, :128]], axis=0)
                        back += dot_nn(window(dx, 2 * od + o_r), band)
                delta1 = back * slope1[pd, pr]
                d1t[:, pl.ds(512 * pd + 256 * pr, 256)] = delta1.T.astype(BF16)

        lane = lax.broadcasted_iota(jnp.int32, (64, 256), 1)
        tiles = [jnp.zeros((64, 128), F32) for _ in range(8)]
        for ab in range(9):
            a, b = divmod(ab, 3)
            grad = jnp.zeros((128, 256), F32)
            for pd in range(2):
                for pr in range(2):
                    grad += dot_nn(
                        d1t[:, pl.ds(512 * pd + 256 * pr, 256)], window(f_ref, 2 * pd + a, 2 * pr + b)
                    )
            both = grad[:64] + pltpu.roll(grad[64:], 256 - 64, 1)
            both = jnp.where((lane >= 96) & (lane < 192), both, 0.0)
            tile, off = divmod(ab * 96, 128)
            both = pltpu.roll(both, (off - 96) % 256, 1)
            tiles[tile] = tiles[tile] + both[:, :128]
            tiles[tile + 1] = tiles[tile + 1] + both[:, 128:]
        for t in range(7):
            acc[pl.ds(1792 + 64 * t, 64), :] = tiles[t]
        acc[pl.ds(2240, 64), :] = jnp.zeros((64, 128), F32)

        def remote(index, src, dst, dev):
            return pltpu.make_async_remote_copy(
                src_ref=src, dst_ref=dst, send_sem=sum_send.at[index], recv_sem=sum_recv.at[index],
                device_id=dev, device_id_type=MESH,
            )

        rows = n_plane * chunk
        other = pl.multiple_of((1 - core) * rows, 8)
        mine = pl.multiple_of(core * rows, 8)
        send1[...] = acc[pl.ds(other, rows), :].reshape(n_plane, chunk, 128).astype(LINK)
        swap = remote(0, send1, recv1, mate)
        swap.start()
        swap.wait()
        summed = acc[pl.ds(mine, rows), :].reshape(n_plane, chunk, 128) + recv1[...].astype(F32)
        half[...] = summed
        send2[...] = summed.astype(LINK)
        base = 1
        copies = []
        for s in range(1, n_plane):
            target = lax.rem(plane + s, n_plane)
            copies.append(remote(base + s, send2.at[target], recv2.at[s], plane_dev(target)))
            copies[-1].start()
        total = half[plane]
        for s in range(1, n_plane):
            copies[s - 1].wait()
            total += recv2[s].astype(F32)
        part[...] = total
        base += n_plane
        copies = []
        for k in range(n_col):
            send3[k] = part[pl.ds(k, piece, stride=n_col), :]
        for s in range(1, n_col):
            target = lax.rem(col + s, n_col)
            copies.append(remote(base + s, send3.at[target], recv3.at[s], (dep, row, target)))
            copies[-1].start()
        total = send3[col]
        for s in range(1, n_col):
            copies[s - 1].wait()
            total += recv3[s]
        tot[...] = total
        recv4[col] = total
        base += n_col
        copies = []
        for s in range(1, n_col):
            target = lax.rem(col + s, n_col)
            copies.append(remote(base + s, tot, recv4.at[col], (dep, row, target)))
            copies[-1].start()
        for copy in copies:
            copy.wait()
        for k in range(n_col):
            part[pl.ds(k, piece, stride=n_col), :] = recv4[k]
        base += n_col
        gath[core, plane] = part[...].astype(LINK)
        copies, onward = [], []
        own = gath.at[core, plane]
        for s in range(1, n_plane):
            target = lax.rem(plane + s, n_plane)
            copies.append(remote(base + s, own, own, plane_dev(target)))
            copies[-1].start()
        base += n_plane
        onward.append(remote(base, own, own, mate))
        onward[-1].start()
        for s in range(1, n_plane):
            copies[s - 1].wait()
            came = gath.at[core, lax.rem(plane - s + n_plane, n_plane)]
            onward.append(remote(base + s, came, came, mate))
            onward[-1].start()
        for copy in onward:
            copy.wait()
        for h in range(2):
            for w in range(n_plane):
                full[pl.ds((h * n_plane + w) * chunk, chunk), :] = gath[h, w].astype(F32)
        for t in range(13):
            g2_out[:, pl.ds(128 * t, 128)] = full[pl.ds(128 * t, 128), :]
        g2_out[:, pl.ds(1664, 64)] = full[pl.ds(1664, 128), pl.ds(0, 64)]
        for t in range(6):
            g1_out[:, pl.ds(128 * t, 128)] = full[pl.ds(1792 + 64 * t, 64), :]
        g1_out[:, pl.ds(768, 96)] = full[pl.ds(1792 + 384, 64), pl.ds(0, 96)]

    return kernel


def solution(mesh):
    n_dep, n_row, n_col = mesh.shape["depth"], mesh.shape["row"], mesh.shape["col"]
    n_plane = n_dep * n_row // 2
    chunk = ROWS // (2 * n_plane)
    piece = chunk // n_col
    kernel = make_kernel(n_dep, n_row, n_col)
    n_sum = 1 + 3 * n_plane + 2 * n_col + 8

    def vm(shape, dtype):
        return pltpu.VMEM(shape, dtype)

    def shards(volume, first_weight, second_weight, cotangent):
        volume = volume.reshape(8, 4, 16, 1024)
        return tuple(pl.pallas_call(
            kernel,
            out_shape=(
                jax.ShapeDtypeStruct((64, 864), F32),
                jax.ShapeDtypeStruct((128, 1728), F32),
            ),
            in_specs=[pl.BlockSpec(memory_space=pltpu.VMEM)] * 4,
            out_specs=(pl.BlockSpec(memory_space=pltpu.VMEM),) * 2,
            scratch_shapes=[
                vm((4, 9, 152, 128), F32), vm((5, 5, 9, 32, 128), BF16),
                vm((64, 896), F32), vm((128, 1792), F32),
                vm((9, 128, 256), BF16), vm((9, 128, 256), BF16), vm((8, 32, 128), F32),
                vm((8, 32, 128), BF16), vm((8, 4, 16, 128), BF16), vm((9, 32, 128), BF16),
                vm((16, 1024), BF16), vm((16, 128), BF16), vm((16, 1024), BF16), vm((16, 128), BF16),
                vm((2, 2, 9, 40, 128), F32), vm((9, 9, 32, 128), BF16), vm((2, 2, 256, 128), F32),
                vm((4, 32, 128), BF16), vm((8, 16, 128), BF16), vm((8, 16, 128), BF16),
                vm((4, 32, 128), BF16), vm((9, 16, 128), BF16), vm((9, 16, 128), BF16), vm((9, 16, 128), BF16),
                vm((9, 40, 128), F32), vm((4, 9, 32, 128), BF16), vm((128, 256), BF16), vm((128, 1024), BF16),
                vm((32, 128), BF16), vm((8, 8, 128), F32), vm((8, 8, 128), F32),
                vm((32, 128), BF16), vm((9, 8, 128), F32), vm((9, 8, 128), F32), vm((9, 8, 128), F32),
                vm((ROWS, 128), F32), vm((n_plane, chunk, 128), F32),
                vm((n_plane, chunk, 128), LINK), vm((n_plane, chunk, 128), LINK),
                vm((n_plane, chunk, 128), LINK), vm((n_plane, chunk, 128), LINK),
                vm((chunk, 128), F32), vm((n_col, piece, 128), F32), vm((n_col, piece, 128), F32),
                vm((piece, 128), F32), vm((n_col, piece, 128), F32),
                vm((2, n_plane, chunk, 128), LINK), vm((ROWS, 128), F32),
                pltpu.SemaphoreType.DMA((21,)), pltpu.SemaphoreType.DMA((21,)),
                pltpu.SemaphoreType.DMA((n_sum + n_plane,)), pltpu.SemaphoreType.DMA((n_sum + n_plane,)),
            ],
            compiler_params=pltpu.CompilerParams(
                collective_id=0, has_side_effects=True, vmem_limit_bytes=48 * 1024 * 1024
            ),
            name="sections",
        )(volume, first_weight, second_weight, cotangent))

    placed = (P("depth", "row", "col"), P(), P(), P("depth", "row", "col"))
    return jax.shard_map(shards, mesh=mesh, in_specs=placed, out_specs=(P(), P()), check_vma=False)
```

profile of v0, /device:TPU:1, one launch (start us, length us, event | category | flops | bytes accessed | tf_op | source)
XLA Modules:
  0.0 61.7 jit_solution(6334295811451512110)
XLA Ops:
  0.6 0.0 copy-start.1
  0.6 0.0 copy-start.2
  0.7 1.3 %copy.6.w2 = bf16[128,1728]{1,0:T(8,128)(2,1)S(1)} copy(bf16[128,1728]{0,1:T(8,128)(2,1)} %param.6) | data formatting | bytes 884736 | tf_op args[2]
  1.9 0.0 copy-done.1
  1.9 0.0 copy-done.2
  1.9 0.0 copy-start
  1.9 1.2 %copy-done = bf16[32,16,1024]{2,1,0:T(8,128)(2,1)S(1)} copy-done((bf16[32,16,1024]{2,1,0:T(8,128)(2,1)S(1)}, bf16[32,16,1024]{2,1,0:T(8,128)(2,1)}, u32[]{:S(2)}) %copy-start) | copy-done | bytes 1048600
  3.2 56.7 %sections.1 = (f32[64,864]{1,0:T(8,128)S(1)}, f32[128,1728]{1,0:T(8,128)S(1)}) custom-call(bf16[8,4,16,1024]{3,2,1,0:T(8,128)(2,1)S(1)} %bitcast.1, bf16[64,864]{1,0:T(8,128)(2,1)S(1)} %copy-done.1, bf16[128,1728]{1,0:T(8,128)(2,1)S(1)} %copy.6.w2, bf16[8,4,1024]{2,1,0:T(4,128)(2,1)S(1)} %copy-done.2), custom_call_target="tpu_custom_call" | custom-call | tf_op jit(solution)/shard_map/sections/pallas_call | solution.py:426
  59.8 1.2 %copy.7 = f32[128,1728]{0,1:T(8,128)} copy(f32[128,1728]{1,0:T(8,128)S(1)} %get-tuple-element.3) | data formatting | bytes 1769472 | tf_op jit(solution)/shard_map/sections/pallas_call | solution.py:426
  61.0 0.7 %copy.9 = f32[64,864]{1,0:T(8,128)} copy(f32[64,864]{1,0:T(8,128)S(1)} %get-tuple-element.6) | data formatting | bytes 442368
Async XLA Ops:
  0.6 1.3 %copy-start.1 = (bf16[64,864]{1,0:T(8,128)(2,1)S(1)}, bf16[64,864]{1,0:T(8,128)(2,1)}, u32[]{:S(2)}) copy-start(bf16[64,864]{1,0:T(8,128)(2,1)} %w1.1) | copy-start | bytes 331780
  0.6 1.3 %copy-start.2 = (bf16[8,4,1024]{2,1,0:T(4,128)(2,1)S(1)}, bf16[8,4,1024]{2,1,0:T(4,128)(2,1)}, u32[]{:S(2)}) copy-start(bf16[8,4,1024]{2,1,0:T(4,128)(2,1)} %cot.1) | copy-start | bytes 196612
  1.9 1.2 %copy-start = (bf16[32,16,1024]{2,1,0:T(8,128)(2,1)S(1)}, bf16[32,16,1024]{2,1,0:T(8,128)(2,1)}, u32[]{:S(2)}) copy-start(bf16[32,16,1024]{2,1,0:T(8,128)(2,1)} %param.4) | copy-start | bytes 3145732
where the time goes:
time: 61.9 us; the launch traced here: 61.7 us
  Pallas kernels  56.7 us (92%)
  local copies, waits for them, and re-layouts  4.38 us (7%)
  between operations  0.68 us (1%)
    pallas_call x1, Pallas kernels, shards(): pl.pallas_call(kernel, out_shape=(jax.ShapeDtypeStruct((64, 864), F32), j...  56.7 us
    unnamed x8, local copies, waits for them, and re-layouts  3.17 us

commit v1 on v0

v1 whole, which is shorter than its diff:
```python
import jax
import jax.numpy as jnp
from jax import lax
from jax.experimental import pallas as pl
from jax.experimental.pallas import tpu as pltpu
from jax.sharding import PartitionSpec as P

MESH = pl.DeviceIdType.MESH
F32 = jnp.float32
BF16 = jnp.bfloat16

ROWS1, ROWS2 = 512, 1792


def leaky(values):
    root = lax.rsqrt(values * values + 1.0)
    return 0.6 * values + 0.4 * ((values * values + 1.0) * root - 1.0)


def leaky_slope(values):
    return 0.6 + 0.4 * values * lax.rsqrt(values * values + 1.0)


def dot_nt(lhs, rhs):
    return lax.dot_general(lhs, rhs, (((1,), (1,)), ((), ())), preferred_element_type=F32)


def dot_tn(lhs, rhs):
    return lax.dot_general(lhs, rhs, (((0,), (0,)), ((), ())), preferred_element_type=F32)


def dot_nn(lhs, rhs):
    return lax.dot_general(lhs, rhs, (((1,), (0,)), ((), ())), preferred_element_type=F32)


def window(ref, *lead):
    low = ref[lead + (pl.ds(0, 8),)].reshape(256, 128)
    high = ref[lead + (pl.ds(1, 8),)].reshape(256, 128)
    return jnp.concatenate([low, high], axis=1)


def make_kernel(n_dep, n_row, n_col):
    n_half = n_row // 2
    n_plane = n_dep * n_half

    def kernel(
        vol_in, w1_in, w2_in, cot_in, g1_out, g2_out,
        vol, w1, w2, cot, load_sem,
        s_ref, f_ref, w1f, w1b, w2b, up,
        f_sc, f_sr, f_sk, f_c, f_r, f_d, f_dc, f_dr, f_drc,
        hs, hx, slope1, h_sc, h_sr, h_sd, h_sk, h_c, h_r, h_d, h_dc, h_dr, h_drc,
        q_ref, dx, d1t, q_sc, q_sr, q_sd, q_sk, q_c, q_r, q_rc, q_d, q_dc, q_dr, q_drc,
        acc1, swap1, send1, come1, cols1, gath1, full1,
        acc2, swap2, send2, come2, cols2, gath2,
        halo_send, halo_recv, sum_send1, sum_recv1, sum_send2, sum_recv2,
    ):
        dep, row, col = lax.axis_index("depth"), lax.axis_index("row"), lax.axis_index("col")
        core, line = lax.rem(row, 2), lax.div(row, 2)
        plane = dep * n_half + line

        loads = [
            pltpu.make_async_copy(src, dst, load_sem.at[i])
            for i, (src, dst) in enumerate(((vol_in, vol), (w1_in, w1), (w2_in, w2), (cot_in, cot)))
        ]
        for load in loads:
            load.start()

        def plane_dev(index):
            return (lax.div(index, n_half), 2 * lax.rem(index, n_half) + core, col)

        def shifted(step, d, r, c):
            return (
                lax.rem(dep + d * step + n_dep, n_dep),
                lax.rem(row + r * step + n_row, n_row),
                lax.rem(col + c * step + n_col, n_col),
            )

        mate = (dep, row + 1 - 2 * core, col)
        corners = [(d, r, c) for d in (0, 1) for r in (0, 1) for c in (0, 1)][1:]

        barrier = pltpu.get_barrier_semaphore()
        peers = [shifted(s, *e) for e in corners for s in (1, -1)]
        peers.append(mate)
        peers += [plane_dev(lax.rem(plane + s, n_plane)) for s in range(1, n_plane)]
        peers += [(dep, row, lax.rem(col + s, n_col)) for s in range(1, n_col)]
        for peer in peers:
            pl.semaphore_signal(barrier, inc=1, device_id=peer, device_id_type=MESH)

        loads[0].wait()
        for rd in range(4):
            for t in (7, 0, 1, 2, 3, 4, 5, 6):
                s_ref[rd, 1 + t, pl.ds(24, 128), :] = (
                    vol[:, rd, :, pl.ds(128 * t, 128)].astype(F32).reshape(128, 128)
                )
        for t in range(8):
            rows = [s_ref[rd, 1 + t, pl.ds(24 + 15, 8, stride=16), :] for rd in range(4)]
            f_sr[t] = jnp.concatenate(rows, axis=0).astype(BF16)
        lane = lax.broadcasted_iota(jnp.int32, (128, 128), 1)
        packed = s_ref[3, 8, pl.ds(24, 128), :]
        for rd in range(3):
            moved = pltpu.roll(s_ref[rd, 8, pl.ds(24, 128), :], 32 * rd + 32, 1)
            packed = jnp.where((lane >= 32 * rd) & (lane < 32 * rd + 32), moved, packed)
        f_sc[...] = packed.astype(BF16)
        for t in range(8):
            f_sk[pl.ds(t, 1), :] = s_ref[3, 1 + t, pl.ds(151, 1), :]

        pl.semaphore_wait(barrier, len(peers))

        def halo(phase, kind, src, dst, step):
            index = phase * 7 + kind
            return pltpu.make_async_remote_copy(
                src_ref=src, dst_ref=dst, send_sem=halo_send.at[index], recv_sem=halo_recv.at[index],
                device_id=shifted(step, *corners[kind]), device_id_type=MESH,
            )

        field_copies = [
            halo(0, 6, f_sc.at[pl.ds(112, 16)], f_drc, 1),
            halo(0, 5, f_sk, f_dr, 1),
            halo(0, 3, vol.at[7, 3], f_d, 1),
            halo(0, 4, f_sc.at[pl.ds(112, 16)], f_dc, 1),
            halo(0, 1, f_sr, f_r.at[pl.ds(1, 8)], 1),
            halo(0, 2, f_sr.at[7], f_r.at[0], 1),
            halo(0, 0, f_sc, f_c, 1),
        ]
        for copy in field_copies:
            copy.start()

        for load in loads[1:]:
            load.wait()
        w1f[:, pl.ds(768, 128)] = jnp.zeros((64, 128), F32)
        w1f[:, pl.ds(0, 864)] = w1[...].astype(F32)
        lane1 = lax.broadcasted_iota(jnp.int32, (64, 256), 1)
        for ab in range(9):
            tile, off = divmod(ab * 96, 128)
            if tile == 6:
                band = jnp.concatenate([w1f[:, pl.ds(768, 128)], jnp.zeros((64, 128), F32)], axis=1)
            else:
                band = w1f[:, pl.ds(128 * tile, 256)]
            for kk, start in ((0, 96), (1, 160)):
                moved = pltpu.roll(band, (start - off) % 256, 1)
                keep = (lane1 >= start) & (lane1 < start + 96)
                w1b[ab, pl.ds(64 * kk, 64), :] = jnp.where(keep, moved, 0.0).astype(BF16)
            w2b[ab, pl.ds(0, 64), :] = jnp.zeros((64, 128), BF16)
            w2b[ab, pl.ds(64, 192), :] = w2[pl.ds(192 * ab, 192), :]
        for i in range(8):
            line_up = cot[i].astype(F32)
            for k in range(8):
                up[k, pl.ds(4 * i, 4), :] = line_up[:, 128 * k : 128 * (k + 1)]

        def pick_field(t, rd, rr):
            source, start = (3, 8) if rd < 0 else (rd, 24)
            rows = s_ref[source, t, pl.ds(start + rr, 32, stride=4), :]
            f_ref[rd + 1, rr + 1, t] = rows.astype(BF16)

        def local_tile(t, carry):
            for rd in range(4):
                for rr in range(4):
                    pick_field(t, rd, rr)
            return carry

        lax.fori_loop(1, 9, local_tile, 0)

        for copy in field_copies:
            copy.wait_recv()

        first_dep, first_row, first_col = dep == 0, row == 0, col == 0

        def unless(edge, values):
            return jnp.where(edge, 0.0, values.astype(F32))

        packed = unless(first_col, f_c[...])
        for rd in range(4):
            s_ref[rd, 0, pl.ds(24, 128), :] = packed if rd == 3 else pltpu.roll(packed, 96 - 32 * rd, 1)
        for t in range(8):
            s_ref[3, 1 + t, pl.ds(8, 16), :] = unless(first_dep, f_d[:, pl.ds(128 * t, 128)])
        s_ref[3, 0, pl.ds(8, 16), :] = unless(first_dep | first_col, f_dc[...])
        for rd in range(4):
            for rr in range(4):
                pick_field(0, rd, rr)

        def above_tile(t, carry):
            for rr in range(4):
                pick_field(t, -1, rr)
            return carry

        lax.fori_loop(0, 9, above_tile, 0)

        def row_tile(t, carry):
            block = unless(first_row | (first_col & (t == 0)), f_r[t])
            for rd in range(4):
                s_ref[rd, t, pl.ds(23, 8, stride=16), :] = block[8 * rd : 8 * rd + 8]
            return carry

        lax.fori_loop(0, 9, row_tile, 0)
        s_ref[3, 0, pl.ds(7, 1), :] = unless(first_dep | first_row | first_col, f_drc[...])[15:16]
        block = unless(first_dep | first_row, f_dr[...])
        for t in range(8):
            s_ref[3, 1 + t, pl.ds(7, 1), :] = block[t : t + 1]

        def behind_tile(t, carry):
            for rd in range(-1, 4):
                pick_field(t, rd, -1)
            return carry

        lax.fori_loop(0, 9, behind_tile, 0)

        for pd in range(2):
            for pr in range(2):
                pre = jnp.zeros((256, 128), F32)
                for ab in range(9):
                    a, b = divmod(ab, 3)
                    pre += dot_nt(window(f_ref, 2 * pd + a, 2 * pr + b), w1b[ab])
                slope1[pd, pr] = leaky_slope(pre)
                hid = leaky(pre).reshape(8, 32, 128)
                hs[pd, pr, pl.ds(1, 8), pl.ds(8, 32), :] = hid
                h_sc[2 * pd + pr] = hid[7].astype(BF16)
        for t in range(8):
            rows = [hs[pd, 1, 1 + t, pl.ds(11, 8, stride=4), :] for pd in range(2)]
            h_sr[t] = jnp.concatenate(rows, axis=0).astype(BF16)
            h_sk[pl.ds(t, 1), :] = hs[1, 1, 1 + t, pl.ds(39, 1), :]
        for t in range(4):
            rows = [hs[1, pr, 1 + 2 * t + u, pl.ds(36, 4), :] for u in range(2) for pr in range(2)]
            h_sd[t] = jnp.concatenate(rows, axis=0).astype(BF16)
        hidden_copies = [
            halo(1, 6, h_sd.at[3], h_drc, 1),
            halo(1, 5, h_sk, h_dr, 1),
            halo(1, 3, h_sd, h_d, 1),
            halo(1, 4, h_sd.at[3], h_dc, 1),
            halo(1, 1, h_sr, h_r.at[pl.ds(1, 8)], 1),
            halo(1, 2, h_sr.at[7], h_r.at[0], 1),
            halo(1, 0, h_sc, h_c, 1),
        ]
        for copy in hidden_copies:
            copy.start()

        def pick_hidden(a, b, pd, pr, start):
            hx[3 * a + b] = hs[pd, pr, :, pl.ds(start, 32), :].astype(BF16)

        for copy in hidden_copies:
            copy.wait_recv()
        for pd in range(2):
            for pr in range(2):
                hs[pd, pr, 0, pl.ds(8, 32), :] = unless(first_col, h_c[2 * pd + pr])
        for t in range(4):
            block = unless(first_dep, h_d[t])
            for u in range(2):
                for pr in range(2):
                    start = 8 * u + 4 * pr
                    hs[1, pr, 1 + 2 * t + u, pl.ds(4, 4), :] = block[start : start + 4]
        block = unless(first_dep | first_col, h_dc[...])
        for pr in range(2):
            hs[1, pr, 0, pl.ds(4, 4), :] = block[8 + 4 * pr : 12 + 4 * pr]
        for pr in range(2):
            pick_hidden(0, 1 + pr, 1, pr, 4)
            pick_hidden(1, 1 + pr, 0, pr, 8)
            pick_hidden(2, 1 + pr, 1, pr, 8)
        for t in range(9):
            edge = first_row | first_col if t == 0 else first_row
            block = unless(edge, h_r[t])
            for pd in range(2):
                hs[pd, 1, t, pl.ds(7, 8, stride=4), :] = block[8 * pd : 8 * pd + 8]
        block = unless(first_dep | first_row, h_dr[...])
        for t in range(8):
            hs[1, 1, 1 + t, pl.ds(3, 1), :] = block[t : t + 1]
        hs[1, 1, 0, pl.ds(3, 1), :] = unless(first_dep | first_row | first_col, h_drc[...])[15:16]
        pick_hidden(0, 0, 1, 1, 3)
        pick_hidden(1, 0, 0, 1, 7)
        pick_hidden(2, 0, 1, 1, 7)

        pre = jnp.zeros((256, 128), F32)
        for ab in range(9):
            pre += dot_nn(window(hx, ab), w2b[ab])
        delta2 = up[...].reshape(256, 128) * leaky_slope(pre)
        q_ref[pl.ds(0, 8), pl.ds(0, 32), :] = delta2.reshape(8, 32, 128)
        q_sc[...] = delta2[:32].astype(BF16)
        for t in range(4):
            rows = [q_ref[2 * t + u, pl.ds(0, 8, stride=4), :] for u in range(2)]
            q_sr[t] = jnp.concatenate(rows, axis=0).astype(BF16)
            rows = [q_ref[2 * t + u, pl.ds(0, 8), :] for u in range(2)]
            q_sd[t] = jnp.concatenate(rows, axis=0).astype(BF16)
        for t in range(8):
            q_sk[pl.ds(t, 1), :] = q_ref[t, pl.ds(0, 1), :]
        delta_copies = [
            halo(2, 6, q_sd.at[0], q_drc, -1),
            halo(2, 5, q_sk, q_dr, -1),
            halo(2, 3, q_sd, q_d, -1),
            halo(2, 4, q_sd.at[0], q_dc, -1),
            halo(2, 1, q_sr, q_r, -1),
            halo(2, 2, q_sr.at[0], q_rc, -1),
            halo(2, 0, q_sc, q_c, -1),
        ]
        for copy in delta_copies:
            copy.start()

        def summing(rows, acc, swap, send, come, cols, gath, sems_out, sems_in):
            half, chunk = rows // 2, rows // (2 * n_plane)

            def remote(index, src, dst, dev):
                return pltpu.make_async_remote_copy(
                    src_ref=src, dst_ref=dst, send_sem=sems_out.at[index], recv_sem=sems_in.at[index],
                    device_id=dev, device_id_type=MESH,
                )

            order = sorted(range(1, n_plane), key=lambda s: -min(s % n_half, n_half - s % n_half))
            other = pl.multiple_of((1 - core) * half, 8)
            mine = pl.multiple_of(core * half, 8)
            first = remote(0, acc.at[pl.ds(other, half)], swap, mate)
            spread, around, back, onward = {}, {}, {}, {}
            own = gath.at[core, plane]
            for s in order:
                target = lax.rem(plane + s, n_plane)
                spread[s] = remote(s, send.at[target], come.at[s], plane_dev(target))
                back[s] = remote(n_plane + s, own, own, plane_dev(target))
                came = gath.at[core, lax.rem(plane - s + n_plane, n_plane)]
                onward[s] = remote(2 * n_plane + s, came, came, mate)
            onward[0] = remote(2 * n_plane, own, own, mate)
            for s in range(1, n_col):
                target = lax.rem(col + s, n_col)
                around[s] = remote(3 * n_plane + s, cols.at[col], cols.at[col], (dep, row, target))

            def to_plane():
                first.wait_recv()
                summed = acc[pl.ds(mine, half), :] + swap[...]
                send[...] = summed.reshape(n_plane, chunk, 128).astype(BF16)
                for s in order:
                    spread[s].start()

            def to_column():
                place = pl.multiple_of(plane * chunk, 8)
                total = acc[pl.ds(mine + place, chunk), :] + swap[pl.ds(place, chunk), :]
                for s in reversed(order):
                    spread[s].wait_recv()
                    total += come[s].astype(F32)
                cols[col] = total.astype(BF16)
                for s in sorted(around, key=lambda s: -min(s, n_col - s)):
                    around[s].start()

            def to_all():
                for s in around:
                    around[s].wait_recv()
                total = cols[0].astype(F32)
                for k in range(1, n_col):
                    total += cols[k].astype(F32)
                gath[core, plane] = total.astype(BF16)
                for s in order:
                    back[s].start()
                onward[0].start()

            def to_mate():
                for s in reversed(order):
                    back[s].wait_recv()
                    onward[s].start()

            def finish():
                for s in onward:
                    onward[s].wait_recv()

            def drain():
                first.wait_send()
                for group in (spread, around, back, onward):
                    for s in group:
                        group[s].wait_send()

            return first.start, to_plane, to_column, to_all, to_mate, finish, drain

        sum1 = summing(ROWS1, acc1, swap1, send1, come1, cols1, gath1, sum_send1, sum_recv1)
        sum2 = summing(ROWS2, acc2, swap2, send2, come2, cols2, gath2, sum_send2, sum_recv2)

        flat2 = delta2.astype(BF16)
        for ab in range(9):
            acc2[pl.ds(192 * ab, 192), :] = dot_tn(window(hx, ab), flat2)[64:]
        acc2[pl.ds(1728, 64), :] = jnp.zeros((64, 128), F32)
        sum2[0]()
        sum2[1]()

        for copy in delta_copies:
            copy.wait_recv()
        last_dep, last_row, last_col = dep == n_dep - 1, row == n_row - 1, col == n_col - 1
        q_ref[8, pl.ds(0, 32), :] = unless(last_col, q_c[...])
        for t in range(8):
            u = 8 * (t % 2)
            q_ref[t, pl.ds(32, 4), :] = unless(last_dep, q_d[t // 2])[u : u + 4]
        q_ref[8, pl.ds(32, 4), :] = unless(last_dep | last_col, q_dc[...])[:4]
        dx[0] = q_ref[:, pl.ds(0, 32), :].astype(BF16)
        dx[2] = q_ref[:, pl.ds(4, 32), :].astype(BF16)
        for t in range(8):
            u = 8 * (t % 2)
            q_ref[t, pl.ds(4, 8, stride=4), :] = unless(last_row, q_r[t // 2])[u : u + 8]
        q_ref[8, pl.ds(4, 8, stride=4), :] = unless(last_row | last_col, q_rc[...])[:8]
        block = unless(last_dep | last_row, q_dr[...])
        for t in range(8):
            q_ref[t, pl.ds(36, 1), :] = block[t : t + 1]
        q_ref[8, pl.ds(36, 1), :] = unless(last_dep | last_row | last_col, q_drc[...])[:1]
        dx[1] = q_ref[:, pl.ds(1, 32), :].astype(BF16)
        dx[3] = q_ref[:, pl.ds(5, 32), :].astype(BF16)

        taps = (((1, 0),), ((2, 0), (0, 1)))
        for pd in range(2):
            for pr in range(2):
                back = jnp.zeros((256, 128), F32)
                for a, od in taps[pd]:
                    for b, o_r in taps[pr]:
                        band = jnp.concatenate(
                            [w2b[3 * a + b, pl.ds(128, 128), :], w2b[3 * a + b, pl.ds(0, 128), :]], axis=1
                        )
                        back += dot_nt(window(dx, 2 * od + o_r), band)
                delta1 = back * slope1[pd, pr]
                d1t[:, pl.ds(512 * pd + 256 * pr, 256)] = delta1.T.astype(BF16)

        lane = lax.broadcasted_iota(jnp.int32, (64, 256), 1)
        tiles = [jnp.zeros((64, 128), F32) for _ in range(8)]
        for ab in range(9):
            a, b = divmod(ab, 3)
            grad = jnp.zeros((128, 256), F32)
            for pd in range(2):
                for pr in range(2):
                    grad += dot_nn(
                        d1t[:, pl.ds(512 * pd + 256 * pr, 256)], window(f_ref, 2 * pd + a, 2 * pr + b)
                    )
            both = grad[:64] + pltpu.roll(grad[64:], 256 - 64, 1)
            both = jnp.where((lane >= 96) & (lane < 192), both, 0.0)
            tile, off = divmod(ab * 96, 128)
            both = pltpu.roll(both, (off - 96) % 256, 1)
            tiles[tile] = tiles[tile] + both[:, :128]
            tiles[tile + 1] = tiles[tile + 1] + both[:, 128:]
        for t in range(8):
            acc1[pl.ds(64 * t, 64), :] = tiles[t]

        sum1[0]()
        sum2[2]()
        sum1[1]()
        sum2[3]()
        sum1[2]()
        sum2[4]()
        sum1[3]()
        sum2[5]()
        chunk1, chunk2 = ROWS1 // (2 * n_plane), ROWS2 // (2 * n_plane)
        for h in range(2):
            for w in range(n_plane):
                start = (h * n_plane + w) * chunk2
                size = min(chunk2, 1728 - start)
                if size > 0:
                    g2_out[pl.ds(start, size), :] = gath2[h, w].astype(F32)[:size]
        sum1[4]()
        sum1[5]()
        for h in range(2):
            for w in range(n_plane):
                full1[pl.ds((h * n_plane + w) * chunk1, chunk1), :] = gath1[h, w].astype(F32)
        for t in range(6):
            g1_out[:, pl.ds(128 * t, 128)] = full1[pl.ds(64 * t, 64), :]
        g1_out[:, pl.ds(768, 96)] = full1[pl.ds(384, 64), pl.ds(0, 96)]
        sum1[6]()
        sum2[6]()
        for copy in field_copies + hidden_copies + delta_copies:
            copy.wait_send()

    return kernel


def solution(mesh):
    n_dep, n_row, n_col = mesh.shape["depth"], mesh.shape["row"], mesh.shape["col"]
    n_plane = n_dep * n_row // 2
    kernel = make_kernel(n_dep, n_row, n_col)
    n_sum = 3 * n_plane + n_col

    def vm(shape, dtype):
        return pltpu.VMEM(shape, dtype)

    def sum_scratch(rows):
        half, chunk = rows // 2, rows // (2 * n_plane)
        return [
            vm((rows, 128), F32), vm((half, 128), F32),
            vm((n_plane, chunk, 128), BF16), vm((n_plane, chunk, 128), BF16),
            vm((n_col, chunk, 128), BF16), vm((2, n_plane, chunk, 128), BF16),
        ]

    def shards(volume, first_weight, second_weight, cotangent):
        first_grad, second_grad = pl.pallas_call(
            kernel,
            out_shape=(
                jax.ShapeDtypeStruct((64, 864), F32),
                jax.ShapeDtypeStruct((1728, 128), F32),
            ),
            in_specs=[pl.BlockSpec(memory_space=pltpu.HBM)] * 4,
            out_specs=(pl.BlockSpec(memory_space=pltpu.VMEM),) * 2,
            scratch_shapes=[
                vm((8, 4, 16, 1024), BF16), vm((64, 864), BF16), vm((1728, 128), BF16), vm((8, 4, 1024), BF16),
                pltpu.SemaphoreType.DMA((4,)),
                vm((4, 9, 152, 128), F32), vm((5, 5, 9, 32, 128), BF16),
                vm((64, 896), F32), vm((9, 128, 256), BF16), vm((9, 256, 128), BF16), vm((8, 32, 128), F32),
                vm((128, 128), BF16), vm((8, 32, 128), BF16), vm((8, 128), F32),
                vm((128, 128), BF16), vm((9, 32, 128), BF16), vm((16, 1024), BF16), vm((16, 128), BF16),
                vm((8, 128), F32), vm((16, 128), BF16),
                vm((2, 2, 9, 40, 128), F32), vm((9, 9, 32, 128), BF16), vm((2, 2, 256, 128), F32),
                vm((4, 32, 128), BF16), vm((8, 16, 128), BF16), vm((4, 16, 128), BF16), vm((8, 128), F32),
                vm((4, 32, 128), BF16), vm((9, 16, 128), BF16), vm((4, 16, 128), BF16), vm((16, 128), BF16),
                vm((8, 128), F32), vm((16, 128), BF16),
                vm((9, 40, 128), F32), vm((4, 9, 32, 128), BF16), vm((128, 1024), BF16),
                vm((32, 128), BF16), vm((4, 16, 128), BF16), vm((4, 16, 128), BF16), vm((8, 128), F32),
                vm((32, 128), BF16), vm((4, 16, 128), BF16), vm((16, 128), BF16),
                vm((4, 16, 128), BF16), vm((16, 128), BF16), vm((8, 128), F32), vm((16, 128), BF16),
                *sum_scratch(ROWS1), vm((ROWS1, 128), F32), *sum_scratch(ROWS2),
                pltpu.SemaphoreType.DMA((21,)), pltpu.SemaphoreType.DMA((21,)),
                pltpu.SemaphoreType.DMA((n_sum,)), pltpu.SemaphoreType.DMA((n_sum,)),
                pltpu.SemaphoreType.DMA((n_sum,)), pltpu.SemaphoreType.DMA((n_sum,)),
            ],
            compiler_params=pltpu.CompilerParams(
                collective_id=0, has_side_effects=True, vmem_limit_bytes=48 * 1024 * 1024
            ),
            name="sections",
        )(*[
            pltpu.with_memory_space_constraint(x, pltpu.HBM)
            for x in (volume.reshape(8, 4, 16, 1024), first_weight, second_weight.T, cotangent)
        ])
        return first_grad, second_grad.T

    placed = (P("depth", "row", "col"), P(), P(), P("depth", "row", "col"))
    return jax.shard_map(shards, mesh=mesh, in_specs=placed, out_specs=(P(), P()), check_vma=False)
```

time: 61.9 us -> 51.8 us (0.84)
  Pallas kernels: 56.7 us -> 49.5 us
  local copies, waits for them, and re-layouts: 4.38 us -> 1.6 us
    pallas_call x1, Pallas kernels: 56.7 us -> 49.5 us  [shards(): pl.pallas_call(kernel, out_shape=(jax.ShapeDtypeStruct((64, 864), F32), j...]
    unnamed x8 -> x2, local copies, waits for them, and re-layouts: 3.17 us -> 1.6 us
    pallas_call x1 -> x0, local copies, waits for them, and re-layouts: 1.21 us -> none  [shards(): pl.pallas_call(kernel, out_shape=(jax.ShapeDtypeStruct((64, 864), F32), j...]
where the time goes in v1:
time: 51.8 us; the launch traced here: 51.7 us
  Pallas kernels  49.5 us (96%)
  local copies, waits for them, and re-layouts  1.6 us (3%)
  between operations  0.64 us (1%)
    pallas_call x1, Pallas kernels, shards(): pl.pallas_call(kernel, out_shape=(jax.ShapeDtypeStruct((64, 864), F32), j...  49.5 us
    unnamed x2, local copies, waits for them, and re-layouts  1.6 us

profile of v1, /device:TPU:1, one launch (start us, length us, event | category | flops | bytes accessed | tf_op | source)
XLA Modules:
  0.0 51.7 jit_solution(7458170834411784273)
XLA Ops:
  0.6 49.5 %sections.1 = (f32[64,864]{1,0:T(8,128)S(1)}, f32[1728,128]{1,0:T(8,128)S(1)}) custom-call(bf16[8,4,16,1024]{3,2,1,0:T(8,128)(2,1)} %bitcast.4, bf16[64,864]{1,0:T(8,128)(2,1)} %w1_in.1, bf16[1728,128]{1,0:T(8,128)(2,1)} %bitcast.5, bf16[8,4,1024]{2,1,0:T(4,128)(2,1)} %cot_in.1), custom_call_target="tpu_custom_call" | custom-call | tf_op jit(solution)/shard_map/sections/pallas_call | solution.py:478
  50.1 0.7 %copy.8 = f32[64,864]{1,0:T(8,128)} copy(f32[64,864]{1,0:T(8,128)S(1)} %get-tuple-element.8) | data formatting | bytes 442368
  50.8 0.9 %copy.9 = f32[128,1728]{0,1:T(8,128)} copy(f32[128,1728]{0,1:T(8,128)S(1)} %bitcast.3) | data formatting | bytes 1769472

commit v2 on v1

--- a/solution.py
+++ b/solution.py
@@ -204,34 +204,44 @@
 
         lax.fori_loop(0, 9, behind_tile, 0)
 
-        for pd in range(2):
-            for pr in range(2):
-                pre = jnp.zeros((256, 128), F32)
-                for ab in range(9):
-                    a, b = divmod(ab, 3)
-                    pre += dot_nt(window(f_ref, 2 * pd + a, 2 * pr + b), w1b[ab])
-                slope1[pd, pr] = leaky_slope(pre)
-                hid = leaky(pre).reshape(8, 32, 128)
-                hs[pd, pr, pl.ds(1, 8), pl.ds(8, 32), :] = hid
-                h_sc[2 * pd + pr] = hid[7].astype(BF16)
+        def first_section(pd, pr):
+            pre = jnp.zeros((256, 128), F32)
+            for ab in range(9):
+                a, b = divmod(ab, 3)
+                pre += dot_nt(window(f_ref, 2 * pd + a, 2 * pr + b), w1b[ab])
+            hid = leaky(pre).reshape(8, 32, 128)
+            hs[pd, pr, pl.ds(1, 8), pl.ds(8, 32), :] = hid
+            slope1[pd, pr] = leaky_slope(pre)
+            h_sc[2 * pd + pr] = hid[7].astype(BF16)
+
+        hidden_copies = [
+            halo(1, 6, h_sk, h_drc, 1),
+            halo(1, 5, h_sk, h_dr, 1),
+            halo(1, 1, h_sr, h_r.at[pl.ds(1, 8)], 1),
+            halo(1, 2, h_sr.at[7], h_r.at[0], 1),
+            halo(1, 3, h_sd, h_d, 1),
+            halo(1, 4, h_sd.at[3], h_dc, 1),
+            halo(1, 0, h_sc, h_c, 1),
+        ]
+        first_section(1, 1)
+        for t in range(8):
+            h_sk[pl.ds(t, 1), :] = hs[1, 1, 1 + t, pl.ds(39, 1), :]
+        for copy in hidden_copies[:2]:
+            copy.start()
+        first_section(0, 1)
         for t in range(8):
             rows = [hs[pd, 1, 1 + t, pl.ds(11, 8, stride=4), :] for pd in range(2)]
             h_sr[t] = jnp.concatenate(rows, axis=0).astype(BF16)
-            h_sk[pl.ds(t, 1), :] = hs[1, 1, 1 + t, pl.ds(39, 1), :]
+        for copy in hidden_copies[2:4]:
+            copy.start()
+        first_section(1, 0)
         for t in range(4):
             rows = [hs[1, pr, 1 + 2 * t + u, pl.ds(36, 4), :] for u in range(2) for pr in range(2)]
             h_sd[t] = jnp.concatenate(rows, axis=0).astype(BF16)
-        hidden_copies = [
-            halo(1, 6, h_sd.at[3], h_drc, 1),
-            halo(1, 5, h_sk, h_dr, 1),
-            halo(1, 3, h_sd, h_d, 1),
-            halo(1, 4, h_sd.at[3], h_dc, 1),
-            halo(1, 1, h_sr, h_r.at[pl.ds(1, 8)], 1),
-            halo(1, 2, h_sr.at[7], h_r.at[0], 1),
-            halo(1, 0, h_sc, h_c, 1),
-        ]
-        for copy in hidden_copies:
+        for copy in hidden_copies[4:6]:
             copy.start()
+        first_section(0, 0)
+        hidden_copies[6].start()
 
         def pick_hidden(a, b, pd, pr, start):
             hx[3 * a + b] = hs[pd, pr, :, pl.ds(start, 32), :].astype(BF16)
@@ -262,7 +272,7 @@
         block = unless(first_dep | first_row, h_dr[...])
         for t in range(8):
             hs[1, 1, 1 + t, pl.ds(3, 1), :] = block[t : t + 1]
-        hs[1, 1, 0, pl.ds(3, 1), :] = unless(first_dep | first_row | first_col, h_drc[...])[15:16]
+        hs[1, 1, 0, pl.ds(3, 1), :] = unless(first_dep | first_row | first_col, h_drc[...])[7:8]
         pick_hidden(0, 0, 1, 1, 3)
         pick_hidden(1, 0, 0, 1, 7)
         pick_hidden(2, 0, 1, 1, 7)
@@ -427,12 +437,13 @@
             acc1[pl.ds(64 * t, 64), :] = tiles[t]
 
         sum1[0]()
+        sum1[1]()
         sum2[2]()
-        sum1[1]()
+        sum1[2]()
         sum2[3]()
-        sum1[2]()
+        sum1[3]()
         sum2[4]()
-        sum1[3]()
+        sum1[4]()
         sum2[5]()
         chunk1, chunk2 = ROWS1 // (2 * n_plane), ROWS2 // (2 * n_plane)
         for h in range(2):
@@ -441,7 +452,6 @@
                 size = min(chunk2, 1728 - start)
                 if size > 0:
                     g2_out[pl.ds(start, size), :] = gath2[h, w].astype(F32)[:size]
-        sum1[4]()
         sum1[5]()
         for h in range(2):
             for w in range(n_plane):
@@ -494,7 +504,7 @@
                 vm((2, 2, 9, 40, 128), F32), vm((9, 9, 32, 128), BF16), vm((2, 2, 256, 128), F32),
                 vm((4, 32, 128), BF16), vm((8, 16, 128), BF16), vm((4, 16, 128), BF16), vm((8, 128), F32),
                 vm((4, 32, 128), BF16), vm((9, 16, 128), BF16), vm((4, 16, 128), BF16), vm((16, 128), BF16),
-                vm((8, 128), F32), vm((16, 128), BF16),
+                vm((8, 128), F32), vm((8, 128), F32),
                 vm((9, 40, 128), F32), vm((4, 9, 32, 128), BF16), vm((128, 1024), BF16),
                 vm((32, 128), BF16), vm((4, 16, 128), BF16), vm((4, 16, 128), BF16), vm((8, 128), F32),
                 vm((32, 128), BF16), vm((4, 16, 128), BF16), vm((16, 128), BF16),

time: 51.8 us -> 48.9 us (0.944)
  Pallas kernels: 49.5 us -> 46.6 us
    pallas_call x1, Pallas kernels: 49.5 us -> 46.6 us  [shards(): pl.pallas_call(kernel, out_shape=(jax.ShapeDtypeStruct((64, 864), F32), j...]
where the time goes in v2:
time: 48.9 us; the launch traced here: 48.8 us
  Pallas kernels  46.6 us (95%)
  local copies, waits for them, and re-layouts  1.6 us (3%)
  between operations  0.64 us (1%)
    pallas_call x1, Pallas kernels, shards(): pl.pallas_call(kernel, out_shape=(jax.ShapeDtypeStruct((64, 864), F32), j...  46.6 us
    unnamed x2, local copies, waits for them, and re-layouts  1.6 us

profile of v2, /device:TPU:1, one launch (start us, length us, event | category | flops | bytes accessed | tf_op | source)
XLA Modules:
  0.0 48.8 jit_solution(16603553636059391913)
XLA Ops:
  0.6 46.6 %sections.1 = (f32[64,864]{1,0:T(8,128)S(1)}, f32[1728,128]{1,0:T(8,128)S(1)}) custom-call(bf16[8,4,16,1024]{3,2,1,0:T(8,128)(2,1)} %bitcast.4, bf16[64,864]{1,0:T(8,128)(2,1)} %w1_in.1, bf16[1728,128]{1,0:T(8,128)(2,1)} %bitcast.5, bf16[8,4,1024]{2,1,0:T(4,128)(2,1)} %cot_in.1), custom_call_target="tpu_custom_call" | custom-call | tf_op jit(solution)/shard_map/sections/pallas_call | solution.py:488
  47.2 0.7 %copy.8 = f32[64,864]{1,0:T(8,128)} copy(f32[64,864]{1,0:T(8,128)S(1)} %get-tuple-element.8) | data formatting | bytes 442368
  47.9 0.9 %copy.9 = f32[128,1728]{0,1:T(8,128)} copy(f32[128,1728]{0,1:T(8,128)S(1)} %bitcast.3) | data formatting | bytes 1769472

commit v3 on v2

--- a/solution.py
+++ b/solution.py
@@ -49,7 +49,7 @@
         s_ref, f_ref, w1f, w1b, w2b, up,
         f_sc, f_sr, f_sk, f_c, f_r, f_d, f_dc, f_dr, f_drc,
         hs, hx, slope1, h_sc, h_sr, h_sd, h_sk, h_c, h_r, h_d, h_dc, h_dr, h_drc,
-        q_ref, dx, d1t, q_sc, q_sr, q_sd, q_sk, q_c, q_r, q_rc, q_d, q_dc, q_dr, q_drc,
+        q_ref, dx, g1acc, q_sc, q_sr, q_sd, q_sk, q_c, q_r, q_rc, q_d, q_dc, q_dr, q_drc,
         acc1, swap1, send1, come1, cols1, gath1, full1,
         acc2, swap2, send2, come2, cols2, gath2,
         halo_send, halo_recv, sum_send1, sum_recv1, sum_send2, sum_recv2,
@@ -116,10 +116,10 @@
         field_copies = [
             halo(0, 6, f_sc.at[pl.ds(112, 16)], f_drc, 1),
             halo(0, 5, f_sk, f_dr, 1),
+            halo(0, 4, f_sc.at[pl.ds(112, 16)], f_dc, 1),
             halo(0, 3, vol.at[7, 3], f_d, 1),
-            halo(0, 4, f_sc.at[pl.ds(112, 16)], f_dc, 1),
+            halo(0, 2, f_sr.at[7], f_r.at[0], 1),
             halo(0, 1, f_sr, f_r.at[pl.ds(1, 8)], 1),
-            halo(0, 2, f_sr.at[7], f_r.at[0], 1),
             halo(0, 0, f_sc, f_c, 1),
         ]
         for copy in field_copies:
@@ -160,49 +160,10 @@
 
         lax.fori_loop(1, 9, local_tile, 0)
 
-        for copy in field_copies:
-            copy.wait_recv()
-
         first_dep, first_row, first_col = dep == 0, row == 0, col == 0
 
         def unless(edge, values):
             return jnp.where(edge, 0.0, values.astype(F32))
-
-        packed = unless(first_col, f_c[...])
-        for rd in range(4):
-            s_ref[rd, 0, pl.ds(24, 128), :] = packed if rd == 3 else pltpu.roll(packed, 96 - 32 * rd, 1)
-        for t in range(8):
-            s_ref[3, 1 + t, pl.ds(8, 16), :] = unless(first_dep, f_d[:, pl.ds(128 * t, 128)])
-        s_ref[3, 0, pl.ds(8, 16), :] = unless(first_dep | first_col, f_dc[...])
-        for rd in range(4):
-            for rr in range(4):
-                pick_field(0, rd, rr)
-
-        def above_tile(t, carry):
-            for rr in range(4):
-                pick_field(t, -1, rr)
-            return carry
-
-        lax.fori_loop(0, 9, above_tile, 0)
-
-        def row_tile(t, carry):
-            block = unless(first_row | (first_col & (t == 0)), f_r[t])
-            for rd in range(4):
-                s_ref[rd, t, pl.ds(23, 8, stride=16), :] = block[8 * rd : 8 * rd + 8]
-            return carry
-
-        lax.fori_loop(0, 9, row_tile, 0)
-        s_ref[3, 0, pl.ds(7, 1), :] = unless(first_dep | first_row | first_col, f_drc[...])[15:16]
-        block = unless(first_dep | first_row, f_dr[...])
-        for t in range(8):
-            s_ref[3, 1 + t, pl.ds(7, 1), :] = block[t : t + 1]
-
-        def behind_tile(t, carry):
-            for rd in range(-1, 4):
-                pick_field(t, rd, -1)
-            return carry
-
-        lax.fori_loop(0, 9, behind_tile, 0)
 
         def first_section(pd, pr):
             pre = jnp.zeros((256, 128), F32)
@@ -223,23 +184,69 @@
             halo(1, 4, h_sd.at[3], h_dc, 1),
             halo(1, 0, h_sc, h_c, 1),
         ]
+        field_copies[6].wait_recv()
+        packed = unless(first_col, f_c[...])
+        for rd in range(4):
+            s_ref[rd, 0, pl.ds(24, 128), :] = packed if rd == 3 else pltpu.roll(packed, 96 - 32 * rd, 1)
+        for rd in range(4):
+            for rr in range(4):
+                pick_field(0, rd, rr)
         first_section(1, 1)
         for t in range(8):
             h_sk[pl.ds(t, 1), :] = hs[1, 1, 1 + t, pl.ds(39, 1), :]
         for copy in hidden_copies[:2]:
             copy.start()
+
+        field_copies[2].wait_recv()
+        field_copies[3].wait_recv()
+        for t in range(8):
+            s_ref[3, 1 + t, pl.ds(8, 16), :] = unless(first_dep, f_d[:, pl.ds(128 * t, 128)])
+        s_ref[3, 0, pl.ds(8, 16), :] = unless(first_dep | first_col, f_dc[...])
+
+        def above_tile(t, carry):
+            for rr in range(4):
+                pick_field(t, -1, rr)
+            return carry
+
+        lax.fori_loop(0, 9, above_tile, 0)
         first_section(0, 1)
         for t in range(8):
             rows = [hs[pd, 1, 1 + t, pl.ds(11, 8, stride=4), :] for pd in range(2)]
             h_sr[t] = jnp.concatenate(rows, axis=0).astype(BF16)
         for copy in hidden_copies[2:4]:
             copy.start()
+
+        field_copies[4].wait_recv()
+        field_copies[5].wait_recv()
+
+        def row_tile(t, carry):
+            block = unless(first_row | (first_col & (t == 0)), f_r[t])
+            for rd in range(4):
+                s_ref[rd, t, pl.ds(23, 8, stride=16), :] = block[8 * rd : 8 * rd + 8]
+            for rd in range(4):
+                pick_field(t, rd, -1)
+            return carry
+
+        lax.fori_loop(0, 9, row_tile, 0)
         first_section(1, 0)
         for t in range(4):
             rows = [hs[1, pr, 1 + 2 * t + u, pl.ds(36, 4), :] for u in range(2) for pr in range(2)]
             h_sd[t] = jnp.concatenate(rows, axis=0).astype(BF16)
         for copy in hidden_copies[4:6]:
             copy.start()
+
+        field_copies[0].wait_recv()
+        field_copies[1].wait_recv()
+        s_ref[3, 0, pl.ds(7, 1), :] = unless(first_dep | first_row | first_col, f_drc[...])[15:16]
+        block = unless(first_dep | first_row, f_dr[...])
+        for t in range(8):
+            s_ref[3, 1 + t, pl.ds(7, 1), :] = block[t : t + 1]
+
+        def edge_tile(t, carry):
+            pick_field(t, -1, -1)
+            return carry
+
+        lax.fori_loop(0, 9, edge_tile, 0)
         first_section(0, 0)
         hidden_copies[6].start()
 
@@ -293,10 +300,10 @@
         delta_copies = [
             halo(2, 6, q_sd.at[0], q_drc, -1),
             halo(2, 5, q_sk, q_dr, -1),
+            halo(2, 4, q_sd.at[0], q_dc, -1),
             halo(2, 3, q_sd, q_d, -1),
-            halo(2, 4, q_sd.at[0], q_dc, -1),
+            halo(2, 2, q_sr.at[0], q_rc, -1),
             halo(2, 1, q_sr, q_r, -1),
-            halo(2, 2, q_sr.at[0], q_rc, -1),
             halo(2, 0, q_sc, q_c, -1),
         ]
         for copy in delta_copies:
@@ -383,50 +390,59 @@
         sum2[0]()
         sum2[1]()
 
-        for copy in delta_copies:
-            copy.wait_recv()
         last_dep, last_row, last_col = dep == n_dep - 1, row == n_row - 1, col == n_col - 1
+        taps = (((1, 0),), ((2, 0), (0, 1)))
+
+        def way_back(pd, pr):
+            back = jnp.zeros((256, 128), F32)
+            for a, od in taps[pd]:
+                for b, o_r in taps[pr]:
+                    band = jnp.concatenate(
+                        [w2b[3 * a + b, pl.ds(128, 128), :], w2b[3 * a + b, pl.ds(0, 128), :]], axis=1
+                    )
+                    back += dot_nt(window(dx, 2 * od + o_r), band)
+            delta1 = (back * slope1[pd, pr]).T.astype(BF16)
+            for ab in range(9):
+                a, b = divmod(ab, 3)
+                grad = dot_nn(delta1, window(f_ref, 2 * pd + a, 2 * pr + b))
+                if pd + pr > 0:
+                    grad += g1acc[ab]
+                if pd + pr < 2:
+                    g1acc[ab] = grad
+                else:
+                    yield grad
+
+        delta_copies[6].wait_recv()
         q_ref[8, pl.ds(0, 32), :] = unless(last_col, q_c[...])
+        dx[0] = q_ref[:, pl.ds(0, 32), :].astype(BF16)
+        list(way_back(0, 0))
+        delta_copies[2].wait_recv()
+        delta_copies[3].wait_recv()
         for t in range(8):
             u = 8 * (t % 2)
             q_ref[t, pl.ds(32, 4), :] = unless(last_dep, q_d[t // 2])[u : u + 4]
         q_ref[8, pl.ds(32, 4), :] = unless(last_dep | last_col, q_dc[...])[:4]
-        dx[0] = q_ref[:, pl.ds(0, 32), :].astype(BF16)
         dx[2] = q_ref[:, pl.ds(4, 32), :].astype(BF16)
+        list(way_back(1, 0))
+        delta_copies[4].wait_recv()
+        delta_copies[5].wait_recv()
         for t in range(8):
             u = 8 * (t % 2)
             q_ref[t, pl.ds(4, 8, stride=4), :] = unless(last_row, q_r[t // 2])[u : u + 8]
         q_ref[8, pl.ds(4, 8, stride=4), :] = unless(last_row | last_col, q_rc[...])[:8]
+        dx[1] = q_ref[:, pl.ds(1, 32), :].astype(BF16)
+        list(way_back(0, 1))
+        delta_copies[0].wait_recv()
+        delta_copies[1].wait_recv()
         block = unless(last_dep | last_row, q_dr[...])
         for t in range(8):
             q_ref[t, pl.ds(36, 1), :] = block[t : t + 1]
         q_ref[8, pl.ds(36, 1), :] = unless(last_dep | last_row | last_col, q_drc[...])[:1]
-        dx[1] = q_ref[:, pl.ds(1, 32), :].astype(BF16)
         dx[3] = q_ref[:, pl.ds(5, 32), :].astype(BF16)
-
-        taps = (((1, 0),), ((2, 0), (0, 1)))
-        for pd in range(2):
-            for pr in range(2):
-                back = jnp.zeros((256, 128), F32)
-                for a, od in taps[pd]:
-                    for b, o_r in taps[pr]:
-                        band = jnp.concatenate(
-                            [w2b[3 * a + b, pl.ds(128, 128), :], w2b[3 * a + b, pl.ds(0, 128), :]], axis=1
-                        )
-                        back += dot_nt(window(dx, 2 * od + o_r), band)
-                delta1 = back * slope1[pd, pr]
-                d1t[:, pl.ds(512 * pd + 256 * pr, 256)] = delta1.T.astype(BF16)
 
         lane = lax.broadcasted_iota(jnp.int32, (64, 256), 1)
         tiles = [jnp.zeros((64, 128), F32) for _ in range(8)]
-        for ab in range(9):
-            a, b = divmod(ab, 3)
-            grad = jnp.zeros((128, 256), F32)
-            for pd in range(2):
-                for pr in range(2):
-                    grad += dot_nn(
-                        d1t[:, pl.ds(512 * pd + 256 * pr, 256)], window(f_ref, 2 * pd + a, 2 * pr + b)
-                    )
+        for ab, grad in enumerate(way_back(1, 1)):
             both = grad[:64] + pltpu.roll(grad[64:], 256 - 64, 1)
             both = jnp.where((lane >= 96) & (lane < 192), both, 0.0)
             tile, off = divmod(ab * 96, 128)
@@ -467,6 +483,15 @@
     return kernel
 
 
+def write_out(g1_in, g2_in, g1_out, g2_out, sems):
+    second = pltpu.make_async_copy(g2_in, g2_out, sems.at[1])
+    second.start()
+    first = pltpu.make_async_copy(g1_in, g1_out, sems.at[0])
+    first.start()
+    first.wait()
+    second.wait()
+
+
 def solution(mesh):
     n_dep, n_row, n_col = mesh.shape["depth"], mesh.shape["row"], mesh.shape["col"]
     n_plane = n_dep * n_row // 2
@@ -505,7 +530,7 @@
                 vm((4, 32, 128), BF16), vm((8, 16, 128), BF16), vm((4, 16, 128), BF16), vm((8, 128), F32),
                 vm((4, 32, 128), BF16), vm((9, 16, 128), BF16), vm((4, 16, 128), BF16), vm((16, 128), BF16),
                 vm((8, 128), F32), vm((8, 128), F32),
-                vm((9, 40, 128), F32), vm((4, 9, 32, 128), BF16), vm((128, 1024), BF16),
+                vm((9, 40, 128), F32), vm((4, 9, 32, 128), BF16), vm((9, 128, 256), F32),
                 vm((32, 128), BF16), vm((4, 16, 128), BF16), vm((4, 16, 128), BF16), vm((8, 128), F32),
                 vm((32, 128), BF16), vm((4, 16, 128), BF16), vm((16, 128), BF16),
                 vm((4, 16, 128), BF16), vm((16, 128), BF16), vm((8, 128), F32), vm((16, 128), BF16),
@@ -522,6 +547,17 @@
             pltpu.with_memory_space_constraint(x, pltpu.HBM)
             for x in (volume.reshape(8, 4, 16, 1024), first_weight, second_weight.T, cotangent)
         ])
+        first_grad, second_grad = pl.pallas_call(
+            write_out,
+            out_shape=(
+                jax.ShapeDtypeStruct((64, 864), F32),
+                jax.ShapeDtypeStruct((1728, 128), F32),
+            ),
+            in_specs=[pl.BlockSpec(memory_space=pltpu.VMEM)] * 2,
+            out_specs=(pl.BlockSpec(memory_space=pltpu.HBM),) * 2,
+            scratch_shapes=[pltpu.SemaphoreType.DMA((2,))],
+            name="write_out",
+        )(pltpu.with_memory_space_constraint(first_grad, pltpu.VMEM), pltpu.with_memory_space_constraint(second_grad, pltpu.VMEM))
         return first_grad, second_grad.T
 
     placed = (P("depth", "row", "col"), P(), P(), P("depth", "row", "col"))

time: 48.9 us -> 47.4 us (0.969)
  local copies, waits for them, and re-layouts: 1.6 us -> 0 us
    unnamed x2 -> x0, local copies, waits for them, and re-layouts: 1.6 us -> none
    pallas_call x0 -> x1, Pallas kernels: none -> 1 us  [shards(): pl.pallas_call(write_out, out_shape=(jax.ShapeDtypeStruct((64, 864), F32)...]
    pallas_call x1, Pallas kernels: 46.6 us -> 45.7 us  [shards(): pl.pallas_call(kernel, out_shape=(jax.ShapeDtypeStruct((64, 864), F32), j...]
where the time goes in v3:
time: 47.4 us; the launch traced here: 47.3 us
  Pallas kernels  46.7 us (99%)
  between operations  0.64 us (1%)
    pallas_call x1, Pallas kernels, shards(): pl.pallas_call(kernel, out_shape=(jax.ShapeDtypeStruct((64, 864), F32), j...  45.7 us
    pallas_call x1, Pallas kernels, shards(): pl.pallas_call(write_out, out_shape=(jax.ShapeDtypeStruct((64, 864), F32)...  1 us

profile of v3, /device:TPU:1, one launch (start us, length us, event | category | flops | bytes accessed | tf_op | source)
XLA Modules:
  0.0 47.3 jit_solution(3404056722696320260)
XLA Ops:
  0.6 45.7 %sections.1 = (f32[64,864]{1,0:T(8,128)S(1)}, f32[1728,128]{1,0:T(8,128)S(1)}) custom-call(bf16[8,4,16,1024]{3,2,1,0:T(8,128)(2,1)} %bitcast.3, bf16[64,864]{1,0:T(8,128)(2,1)} %w1_in.1, bf16[1728,128]{1,0:T(8,128)(2,1)} %bitcast.4, bf16[8,4,1024]{2,1,0:T(4,128)(2,1)} %cot_in.1), custom_call_target="tpu_custom_call" | custom-call | tf_op jit(solution)/shard_map/sections/pallas_call | solution.py:513
  46.3 1.0 %write_out.1 = (f32[64,864]{1,0:T(8,128)}, f32[1728,128]{1,0:T(8,128)}) custom-call(f32[64,864]{1,0:T(8,128)S(1)} %get-tuple-element.6.g1_in, f32[1728,128]{1,0:T(8,128)S(1)} %get-tuple-element.7.g2_in), custom_call_target="tpu_custom_call" | custom-call | tf_op jit(solution)/shard_map/write_out/pallas_call | solution.py:550

commit v4 on v3

--- a/solution.py
+++ b/solution.py
@@ -62,8 +62,7 @@
             pltpu.make_async_copy(src, dst, load_sem.at[i])
             for i, (src, dst) in enumerate(((vol_in, vol), (w1_in, w1), (w2_in, w2), (cot_in, cot)))
         ]
-        for load in loads:
-            load.start()
+        loads[0].start()
 
         def plane_dev(index):
             return (lax.div(index, n_half), 2 * lax.rem(index, n_half) + core, col)
@@ -85,6 +84,8 @@
         peers += [(dep, row, lax.rem(col + s, n_col)) for s in range(1, n_col)]
         for peer in peers:
             pl.semaphore_signal(barrier, inc=1, device_id=peer, device_id_type=MESH)
+        for load in loads[1:]:
+            load.start()
 
         loads[0].wait()
         for rd in range(4):
@@ -160,16 +161,36 @@
 
         lax.fori_loop(1, 9, local_tile, 0)
 
+        for rd in range(4):
+            for rr in range(4):
+                f_ref[rd + 1, rr + 1, 0] = jnp.zeros((32, 128), BF16)
+
+        def tap_places(pd, pr, local):
+            for ab in range(9):
+                place = (2 * pd + ab // 3, 2 * pr + ab % 3)
+                if (min(place) > 0) == local:
+                    yield ab, place
+
+        for pd in range(2):
+            for pr in range(2):
+                pre = jnp.zeros((256, 128), F32)
+                for ab, place in tap_places(pd, pr, True):
+                    pre += dot_nt(window(f_ref, *place), w1b[ab])
+                slope1[pd, pr] = pre
+
         first_dep, first_row, first_col = dep == 0, row == 0, col == 0
 
         def unless(edge, values):
             return jnp.where(edge, 0.0, values.astype(F32))
 
         def first_section(pd, pr):
-            pre = jnp.zeros((256, 128), F32)
-            for ab in range(9):
-                a, b = divmod(ab, 3)
-                pre += dot_nt(window(f_ref, 2 * pd + a, 2 * pr + b), w1b[ab])
+            edge = jnp.zeros((32, 128), F32)
+            for ab, place in tap_places(pd, pr, True):
+                edge += dot_nt(f_ref[place + (0,)], w1b[ab, :, pl.ds(0, 128)])
+            pre = slope1[pd, pr]
+            pre = jnp.concatenate([pre[:32] + edge, pre[32:]], axis=0)
+            for ab, place in tap_places(pd, pr, False):
+                pre += dot_nt(window(f_ref, *place), w1b[ab])
             hid = leaky(pre).reshape(8, 32, 128)
             hs[pd, pr, pl.ds(1, 8), pl.ds(8, 32), :] = hid
             slope1[pd, pr] = leaky_slope(pre)
@@ -309,7 +330,7 @@
         for copy in delta_copies:
             copy.start()
 
-        def summing(rows, acc, swap, send, come, cols, gath, sems_out, sems_in):
+        def summing(rows, acc, swap, send, come, cols, gath, sems_out, sems_in, cuts):
             half, chunk = rows // 2, rows // (2 * n_plane)
 
             def remote(index, src, dst, dev):
@@ -319,9 +340,11 @@
                 )
 
             order = sorted(range(1, n_plane), key=lambda s: -min(s % n_half, n_half - s % n_half))
-            other = pl.multiple_of((1 - core) * half, 8)
-            mine = pl.multiple_of(core * half, 8)
-            first = remote(0, acc.at[pl.ds(other, half)], swap, mate)
+            pieces = [(low, high) for low, high in zip((0,) + cuts, cuts + (n_plane,)) if high > low]
+            first = []
+            for i, (low, high) in enumerate(pieces):
+                part = pl.ds(low * chunk, (high - low) * chunk)
+                first.append(remote(3 * n_plane + n_col + i, acc.at[1 - core, part], swap.at[part], mate))
             spread, around, back, onward = {}, {}, {}, {}
             own = gath.at[core, plane]
             for s in order:
@@ -336,15 +359,17 @@
                 around[s] = remote(3 * n_plane + s, cols.at[col], cols.at[col], (dep, row, target))
 
             def to_plane():
-                first.wait_recv()
-                summed = acc[pl.ds(mine, half), :] + swap[...]
-                send[...] = summed.reshape(n_plane, chunk, 128).astype(BF16)
+                for (low, high), copy in zip(pieces, first):
+                    copy.wait_recv()
+                    part = pl.ds(low * chunk, (high - low) * chunk)
+                    summed = acc[core, part, :] + swap[part, :]
+                    send[pl.ds(low, high - low)] = summed.reshape(high - low, chunk, 128).astype(BF16)
                 for s in order:
                     spread[s].start()
 
             def to_column():
                 place = pl.multiple_of(plane * chunk, 8)
-                total = acc[pl.ds(mine + place, chunk), :] + swap[pl.ds(place, chunk), :]
+                total = acc[core, pl.ds(place, chunk), :] + swap[pl.ds(place, chunk), :]
                 for s in reversed(order):
                     spread[s].wait_recv()
                     total += come[s].astype(F32)
@@ -372,22 +397,30 @@
                 for s in onward:
                     onward[s].wait_recv()
 
-            def drain():
-                first.wait_send()
-                for group in (spread, around, back, onward):
+            def drain(*names):
+                for name in names:
+                    group = {"first": dict(enumerate(first)), "spread": spread, "around": around, "back": back, "onward": onward}[name]
                     for s in group:
                         group[s].wait_send()
 
-            return first.start, to_plane, to_column, to_all, to_mate, finish, drain
-
-        sum1 = summing(ROWS1, acc1, swap1, send1, come1, cols1, gath1, sum_send1, sum_recv1)
-        sum2 = summing(ROWS2, acc2, swap2, send2, come2, cols2, gath2, sum_send2, sum_recv2)
+            return list(first), to_plane, to_column, to_all, to_mate, finish, drain
+
+        sum1 = summing(ROWS1, acc1, swap1, send1, come1, cols1, gath1, sum_send1, sum_recv1, ())
+        chunk2 = ROWS2 // (2 * n_plane)
+        sum2 = summing(ROWS2, acc2, swap2, send2, come2, cols2, gath2, sum_send2, sum_recv2, (288 // chunk2, 576 // chunk2))
 
         flat2 = delta2.astype(BF16)
+        acc2[:, pl.ds(864, 32), :] = jnp.zeros((2, 32, 128), F32)
+        ready = 0
         for ab in range(9):
-            acc2[pl.ds(192 * ab, 192), :] = dot_tn(window(hx, ab), flat2)[64:]
-        acc2[pl.ds(1728, 64), :] = jnp.zeros((64, 128), F32)
-        sum2[0]()
+            grad = dot_tn(window(hx, ab), flat2)
+            for h in range(2):
+                acc2[h, pl.ds(96 * ab, 96), :] = grad[64 + 96 * h : 160 + 96 * h]
+            if ab % 3 == 2:
+                whole = n_plane if ab == 8 else 96 * (ab + 1) // chunk2
+                if whole > ready:
+                    sum2[0].pop(0).start()
+                ready = whole
         sum2[1]()
 
         last_dep, last_row, last_col = dep == n_dep - 1, row == n_row - 1, col == n_col - 1
@@ -450,35 +483,51 @@
             tiles[tile] = tiles[tile] + both[:, :128]
             tiles[tile + 1] = tiles[tile + 1] + both[:, 128:]
         for t in range(8):
-            acc1[pl.ds(64 * t, 64), :] = tiles[t]
-
-        sum1[0]()
+            acc1[t // 4, pl.ds(64 * (t % 4), 64), :] = tiles[t]
+
+        def widen2(h):
+            for w in range(n_plane):
+                row = w * chunk2
+                values = gath2[h, w].astype(F32)
+                while row < min((w + 1) * chunk2, 864):
+                    stop = min((row // 96 + 1) * 96, (w + 1) * chunk2, 864)
+                    start = pl.multiple_of(row // 96 * 192 + row % 96 + h * 96, 8)
+                    g2_out[pl.ds(start, stop - row), :] = values[row - w * chunk2 : stop - w * chunk2]
+                    row = stop
+
+        sum1[0][0].start()
+        for copy in field_copies + hidden_copies + delta_copies:
+            copy.wait_send()
         sum1[1]()
         sum2[2]()
+        sum1[6]("first")
+        sum2[6]("first", "spread")
         sum1[2]()
+        sum1[6]("spread")
         sum2[3]()
+        sum2[6]("around")
         sum1[3]()
+        sum1[6]("around")
         sum2[4]()
+        widen2(core)
+        sum2[6]("back")
         sum1[4]()
         sum2[5]()
-        chunk1, chunk2 = ROWS1 // (2 * n_plane), ROWS2 // (2 * n_plane)
-        for h in range(2):
-            for w in range(n_plane):
-                start = (h * n_plane + w) * chunk2
-                size = min(chunk2, 1728 - start)
-                if size > 0:
-                    g2_out[pl.ds(start, size), :] = gath2[h, w].astype(F32)[:size]
+        sum2[6]("onward")
+        widen2(1 - core)
+
+        def widen(h):
+            start = pl.multiple_of(h * (ROWS1 // 2), 8)
+            full1[pl.ds(start, ROWS1 // 2), :] = gath1[h].astype(F32).reshape(ROWS1 // 2, 128)
+
+        widen(core)
+        sum1[6]("back")
         sum1[5]()
-        for h in range(2):
-            for w in range(n_plane):
-                full1[pl.ds((h * n_plane + w) * chunk1, chunk1), :] = gath1[h, w].astype(F32)
+        widen(1 - core)
         for t in range(6):
             g1_out[:, pl.ds(128 * t, 128)] = full1[pl.ds(64 * t, 64), :]
         g1_out[:, pl.ds(768, 96)] = full1[pl.ds(384, 64), pl.ds(0, 96)]
-        sum1[6]()
-        sum2[6]()
-        for copy in field_copies + hidden_copies + delta_copies:
-            copy.wait_send()
+        sum1[6]("onward")
 
     return kernel
 
@@ -496,7 +545,7 @@
     n_dep, n_row, n_col = mesh.shape["depth"], mesh.shape["row"], mesh.shape["col"]
     n_plane = n_dep * n_row // 2
     kernel = make_kernel(n_dep, n_row, n_col)
-    n_sum = 3 * n_plane + n_col
+    n_sum = 3 * n_plane + n_col + 3
 
     def vm(shape, dtype):
         return pltpu.VMEM(shape, dtype)
@@ -504,7 +553,7 @@
     def sum_scratch(rows):
         half, chunk = rows // 2, rows // (2 * n_plane)
         return [
-            vm((rows, 128), F32), vm((half, 128), F32),
+            vm((2, half, 128), F32), vm((half, 128), F32),
             vm((n_plane, chunk, 128), BF16), vm((n_plane, chunk, 128), BF16),
             vm((n_col, chunk, 128), BF16), vm((2, n_plane, chunk, 128), BF16),
         ]

time: 47.4 us -> 46.9 us (0.989)
  Pallas kernels: 46.7 us -> 46.2 us
    pallas_call x1, Pallas kernels: 45.7 us -> 45.2 us  [shards(): pl.pallas_call(kernel, out_shape=(jax.ShapeDtypeStruct((64, 864), F32), j...]
where the time goes in v4:
time: 46.9 us; the launch traced here: 46.8 us
  Pallas kernels  46.2 us (99%)
  between operations  0.64 us (1%)
    pallas_call x1, Pallas kernels, shards(): pl.pallas_call(kernel, out_shape=(jax.ShapeDtypeStruct((64, 864), F32), j...  45.2 us
    pallas_call x1, Pallas kernels, shards(): pl.pallas_call(write_out, out_shape=(jax.ShapeDtypeStruct((64, 864), F32)...  1 us

profile of v4, /device:TPU:1, one launch (start us, length us, event | category | flops | bytes accessed | tf_op | source)
XLA Modules:
  0.0 46.8 jit_solution(5392518611508695306)
XLA Ops:
  0.6 45.2 %sections.1 = (f32[64,864]{1,0:T(8,128)S(1)}, f32[1728,128]{1,0:T(8,128)S(1)}) custom-call(bf16[8,4,16,1024]{3,2,1,0:T(8,128)(2,1)} %bitcast.3, bf16[64,864]{1,0:T(8,128)(2,1)} %w1_in.1, bf16[1728,128]{1,0:T(8,128)(2,1)} %bitcast.4, bf16[8,4,1024]{2,1,0:T(4,128)(2,1)} %cot_in.1), custom_call_target="tpu_custom_call" | custom-call | tf_op jit(solution)/shard_map/sections/pallas_call | solution.py:562
  45.8 1.0 %write_out.1 = (f32[64,864]{1,0:T(8,128)}, f32[1728,128]{1,0:T(8,128)}) custom-call(f32[64,864]{1,0:T(8,128)S(1)} %get-tuple-element.6.g1_in, f32[1728,128]{1,0:T(8,128)S(1)} %get-tuple-element.7.g2_in), custom_call_target="tpu_custom_call" | custom-call | tf_op jit(solution)/shard_map/write_out/pallas_call | solution.py:599

commit v5 on v4

--- a/solution.py
+++ b/solution.py
@@ -107,8 +107,8 @@
 
         pl.semaphore_wait(barrier, len(peers))
 
-        def halo(phase, kind, src, dst, step):
-            index = phase * 7 + kind
+        def halo(phase, kind, src, dst, step, index=None):
+            index = phase * 7 + kind if index is None else index
             return pltpu.make_async_remote_copy(
                 src_ref=src, dst_ref=dst, send_sem=halo_send.at[index], recv_sem=halo_recv.at[index],
                 device_id=shifted(step, *corners[kind]), device_id_type=MESH,
@@ -203,7 +203,10 @@
             halo(1, 2, h_sr.at[7], h_r.at[0], 1),
             halo(1, 3, h_sd, h_d, 1),
             halo(1, 4, h_sd.at[3], h_dc, 1),
-            halo(1, 0, h_sc, h_c, 1),
+            halo(1, 0, h_sc.at[3], h_c.at[3], 1),
+            halo(1, 0, h_sc.at[1], h_c.at[1], 1, 21),
+            halo(1, 0, h_sc.at[2], h_c.at[2], 1, 22),
+            halo(1, 0, h_sc.at[0], h_c.at[0], 1, 23),
         ]
         field_copies[6].wait_recv()
         packed = unless(first_col, f_c[...])
@@ -215,7 +218,7 @@
         first_section(1, 1)
         for t in range(8):
             h_sk[pl.ds(t, 1), :] = hs[1, 1, 1 + t, pl.ds(39, 1), :]
-        for copy in hidden_copies[:2]:
+        for copy in hidden_copies[:2] + hidden_copies[6:7]:
             copy.start()
 
         field_copies[2].wait_recv()
@@ -234,7 +237,7 @@
         for t in range(8):
             rows = [hs[pd, 1, 1 + t, pl.ds(11, 8, stride=4), :] for pd in range(2)]
             h_sr[t] = jnp.concatenate(rows, axis=0).astype(BF16)
-        for copy in hidden_copies[2:4]:
+        for copy in hidden_copies[2:4] + hidden_copies[7:8]:
             copy.start()
 
         field_copies[4].wait_recv()
@@ -253,7 +256,7 @@
         for t in range(4):
             rows = [hs[1, pr, 1 + 2 * t + u, pl.ds(36, 4), :] for u in range(2) for pr in range(2)]
             h_sd[t] = jnp.concatenate(rows, axis=0).astype(BF16)
-        for copy in hidden_copies[4:6]:
+        for copy in hidden_copies[4:6] + hidden_copies[8:9]:
             copy.start()
 
         field_copies[0].wait_recv()
@@ -269,7 +272,7 @@
 
         lax.fori_loop(0, 9, edge_tile, 0)
         first_section(0, 0)
-        hidden_copies[6].start()
+        hidden_copies[9].start()
 
         def pick_hidden(a, b, pd, pr, start):
             hx[3 * a + b] = hs[pd, pr, :, pl.ds(start, 32), :].astype(BF16)
@@ -327,7 +330,7 @@
             halo(2, 1, q_sr, q_r, -1),
             halo(2, 0, q_sc, q_c, -1),
         ]
-        for copy in delta_copies:
+        for copy in reversed(delta_copies):
             copy.start()
 
         def summing(rows, acc, swap, send, come, cols, gath, sems_out, sems_in, cuts):
@@ -570,12 +573,12 @@
             scratch_shapes=[
                 vm((8, 4, 16, 1024), BF16), vm((64, 864), BF16), vm((1728, 128), BF16), vm((8, 4, 1024), BF16),
                 pltpu.SemaphoreType.DMA((4,)),
-                vm((4, 9, 152, 128), F32), vm((5, 5, 9, 32, 128), BF16),
+                vm((4, 9, 168, 128), F32), vm((5, 5, 9, 32, 128), BF16),
                 vm((64, 896), F32), vm((9, 128, 256), BF16), vm((9, 256, 128), BF16), vm((8, 32, 128), F32),
                 vm((128, 128), BF16), vm((8, 32, 128), BF16), vm((8, 128), F32),
                 vm((128, 128), BF16), vm((9, 32, 128), BF16), vm((16, 1024), BF16), vm((16, 128), BF16),
                 vm((8, 128), F32), vm((16, 128), BF16),
-                vm((2, 2, 9, 40, 128), F32), vm((9, 9, 32, 128), BF16), vm((2, 2, 256, 128), F32),
+                vm((2, 2, 9, 48, 128), F32), vm((9, 9, 32, 128), BF16), vm((2, 2, 256, 128), F32),
                 vm((4, 32, 128), BF16), vm((8, 16, 128), BF16), vm((4, 16, 128), BF16), vm((8, 128), F32),
                 vm((4, 32, 128), BF16), vm((9, 16, 128), BF16), vm((4, 16, 128), BF16), vm((16, 128), BF16),
                 vm((8, 128), F32), vm((8, 128), F32),
@@ -584,7 +587,7 @@
                 vm((32, 128), BF16), vm((4, 16, 128), BF16), vm((16, 128), BF16),
                 vm((4, 16, 128), BF16), vm((16, 128), BF16), vm((8, 128), F32), vm((16, 128), BF16),
                 *sum_scratch(ROWS1), vm((ROWS1, 128), F32), *sum_scratch(ROWS2),
-                pltpu.SemaphoreType.DMA((21,)), pltpu.SemaphoreType.DMA((21,)),
+                pltpu.SemaphoreType.DMA((24,)), pltpu.SemaphoreType.DMA((24,)),
                 pltpu.SemaphoreType.DMA((n_sum,)), pltpu.SemaphoreType.DMA((n_sum,)),
                 pltpu.SemaphoreType.DMA((n_sum,)), pltpu.SemaphoreType.DMA((n_sum,)),
             ],

time: 46.9 us -> 47 us (level)
  no operation moved by 1% of the time
where the time goes in v5:
time: 47 us; the launch traced here: 46.9 us
  Pallas kernels  46.3 us (99%)
  between operations  0.64 us (1%)
    pallas_call x1, Pallas kernels, shards(): pl.pallas_call(kernel, out_shape=(jax.ShapeDtypeStruct((64, 864), F32), j...  45.3 us
    pallas_call x1, Pallas kernels, shards(): pl.pallas_call(write_out, out_shape=(jax.ShapeDtypeStruct((64, 864), F32)...  1 us

profile of v5, /device:TPU:1, one launch (start us, length us, event | category | flops | bytes accessed | tf_op | source)
XLA Modules:
  0.0 46.9 jit_solution(2656782330721732297)
XLA Ops:
  0.6 45.3 %sections.1 = (f32[64,864]{1,0:T(8,128)S(1)}, f32[1728,128]{1,0:T(8,128)S(1)}) custom-call(bf16[8,4,16,1024]{3,2,1,0:T(8,128)(2,1)} %bitcast.3, bf16[64,864]{1,0:T(8,128)(2,1)} %w1_in.1, bf16[1728,128]{1,0:T(8,128)(2,1)} %bitcast.4, bf16[8,4,1024]{2,1,0:T(4,128)(2,1)} %cot_in.1), custom_call_target="tpu_custom_call" | custom-call | tf_op jit(solution)/shard_map/sections/pallas_call | solution.py:565
  45.9 1.0 %write_out.1 = (f32[64,864]{1,0:T(8,128)}, f32[1728,128]{1,0:T(8,128)}) custom-call(f32[64,864]{1,0:T(8,128)S(1)} %get-tuple-element.6.g1_in, f32[1728,128]{1,0:T(8,128)S(1)} %get-tuple-element.7.g2_in), custom_call_target="tpu_custom_call" | custom-call | tf_op jit(solution)/shard_map/write_out/pallas_call | solution.py:602

commit v6 on v5

--- a/solution.py
+++ b/solution.py
@@ -512,9 +512,9 @@
         sum1[3]()
         sum1[6]("around")
         sum2[4]()
+        sum1[4]()
         widen2(core)
         sum2[6]("back")
-        sum1[4]()
         sum2[5]()
         sum2[6]("onward")
         widen2(1 - core)

time: 47 us -> 47 us (level)
  no operation moved by 1% of the time
where the time goes in v6:
time: 47 us; the launch traced here: 46.9 us
  Pallas kernels  46.3 us (99%)
  between operations  0.64 us (1%)
    pallas_call x1, Pallas kernels, shards(): pl.pallas_call(kernel, out_shape=(jax.ShapeDtypeStruct((64, 864), F32), j...  45.3 us
    pallas_call x1, Pallas kernels, shards(): pl.pallas_call(write_out, out_shape=(jax.ShapeDtypeStruct((64, 864), F32)...  1 us

profile of v6, /device:TPU:1, one launch (start us, length us, event | category | flops | bytes accessed | tf_op | source)
XLA Modules:
  0.0 46.9 jit_solution(10304345459657736353)
XLA Ops:
  0.6 45.3 %sections.1 = (f32[64,864]{1,0:T(8,128)S(1)}, f32[1728,128]{1,0:T(8,128)S(1)}) custom-call(bf16[8,4,16,1024]{3,2,1,0:T(8,128)(2,1)} %bitcast.3, bf16[64,864]{1,0:T(8,128)(2,1)} %w1_in.1, bf16[1728,128]{1,0:T(8,128)(2,1)} %bitcast.4, bf16[8,4,1024]{2,1,0:T(4,128)(2,1)} %cot_in.1), custom_call_target="tpu_custom_call" | custom-call | tf_op jit(solution)/shard_map/sections/pallas_call | solution.py:565
  45.9 1.0 %write_out.1 = (f32[64,864]{1,0:T(8,128)}, f32[1728,128]{1,0:T(8,128)}) custom-call(f32[64,864]{1,0:T(8,128)S(1)} %get-tuple-element.6.g1_in, f32[1728,128]{1,0:T(8,128)S(1)} %get-tuple-element.7.g2_in), custom_call_target="tpu_custom_call" | custom-call | tf_op jit(solution)/shard_map/write_out/pallas_call | solution.py:602
